TPU v7x, 256 devices: a whole 4x4x8 slice. The times are simulated.
256 devices in a mesh: dp: 32 (over x_lo, z, core), feat: 8 (over x_hi, y).
Axes of the slice: x: 4 (x_hi: 2, x_lo: 2; x = x_hi * 2 + x_lo), y: 4, z: 8, core: 2. Of those that a mesh axis runs over, the one named last changes fastest.
Arguments:
- student: bfloat16 [16384, 2048], P('dp'), may hold values from -6 to 6
- weight: bfloat16 [2048, 4096], P('dp', 'feat'), may hold values from -0.125 to 0.125
- teacher: bfloat16 [16384, 4096], P('dp', 'feat'), may hold values from -6 to 6
Outputs:
- loss: float32 [], replicated
- grad_weight: float32 [2048, 4096], P('dp', 'feat')
All inputs are finite; a program needn't handle non-finite values.
Results may differ from a plain program's by a relative error of at most 0.0022.
The roundings to bfloat16 on the way count: a program that leaves them out, or rounds other values in their place, can miss the bound.
Values may be sent and summed in bfloat16 or wider, within the bound.
A program may use at most 64 MiB of HBM per device.

v0:
```python
import jax
import jax.numpy as jnp
from jax import lax
from jax.sharding import PartitionSpec as P

OFF_WEIGHT = 0.5
NORM_EPS = 1e-05
LOSS_SCALE = 128.0


def apply_norm(values, sums, squares, total):
    center = sums / total
    spread = squares / total - center * center
    recip = lax.rsqrt(spread + NORM_EPS)
    return ((values - center) * recip, recip)


def shards(student, weight, teacher):
    dp_size = lax.axis_size("dp")
    dp_index = lax.axis_index("dp")
    feat_index = lax.axis_index("feat")
    local_rows = student.shape[0]
    total_rows = local_rows * dp_size
    feat_cols = weight.shape[1]
    width_all = feat_cols * lax.axis_size("feat")
    inputs = student
    projected = jnp.dot(
        inputs, lax.all_gather(weight, "dp", axis=0, tiled=True), preferred_element_type=jnp.float32
    )
    proj_sums = jnp.sum(projected, axis=0)
    proj_squares = jnp.sum(projected * projected, axis=0)
    teacher_float = teacher.astype(jnp.float32)
    teach_sums, teach_squares = lax.psum(
        (jnp.sum(teacher_float, axis=0), jnp.sum(teacher_float * teacher_float, axis=0)), "dp"
    )
    teacher_part, teacher_recip = apply_norm(teacher_float, teach_sums, teach_squares, total_rows)
    teacher_normal = lax.all_gather(teacher_part.astype(jnp.bfloat16), "feat", axis=1, tiled=True)
    proj_sums, proj_squares = lax.psum((proj_sums, proj_squares), "dp")
    student_float, recip = apply_norm(projected, proj_sums, proj_squares, total_rows)
    student_normal = student_float.astype(jnp.bfloat16)
    local_corr = lax.dot_general(
        student_normal, teacher_normal, (((0,), (0,)), ((), ())), preferred_element_type=jnp.float32
    )
    share = lax.psum_scatter(local_corr, "dp", scatter_dimension=0, tiled=True) / total_rows
    rows_here = share.shape[0]
    student_index = (
        feat_index * feat_cols
        + dp_index * rows_here
        + lax.broadcasted_iota(jnp.int32, share.shape, 0)
    )
    teacher_index = lax.broadcasted_iota(jnp.int32, share.shape, 1)
    on_diag = student_index == teacher_index
    loss_part = jnp.sum(jnp.where(on_diag, (1.0 - share) ** 2, OFF_WEIGHT * share * share))
    slope = jnp.where(on_diag, -2.0 * (1.0 - share), 2.0 * OFF_WEIGHT * share).astype(jnp.bfloat16)
    loss = lax.psum(loss_part, ("dp", "feat")) / width_all
    upstream = lax.dot_general(
        teacher_normal,
        lax.all_gather(slope, "dp", axis=0, tiled=True),
        (((1,), (1,)), ((), ())),
        preferred_element_type=jnp.float32,
    )
    upstream = upstream / total_rows
    grad_sums, cross_sums = lax.psum(
        (jnp.sum(upstream, axis=0), jnp.sum(upstream * student_float, axis=0)), "dp"
    )
    delta = (
        recip * (upstream - grad_sums / total_rows - student_float * (cross_sums / total_rows))
    ).astype(jnp.bfloat16)
    inputs = student
    grad_weight = LOSS_SCALE * lax.psum_scatter(
        lax.dot_general(
            inputs, delta, (((0,), (0,)), ((), ())), preferred_element_type=jnp.float32
        ),
        "dp",
        scatter_dimension=0,
        tiled=True,
    )
    return (loss, grad_weight)


def solution(mesh):
    placed = (P("dp", None), P("dp", "feat"), P("dp", "feat"))
    return jax.shard_map(
        shards, mesh=mesh, in_specs=placed, out_specs=(P(), P("dp", "feat")), check_vma=False
    )
```

profile of v0, /device:TPU:1, one launch (start us, length us, event | category | flops | bytes accessed | tf_op | source)
XLA Modules:
  0.0 609.8 jit_solution(16516746050749695772)
XLA Ops:
  7.2 0.0 copy-start
  7.2 0.0 all-gather.4.cloned.1.call-start
  7.2 0.7 all-gather.4.cloned.1.call-update
  7.9 0.0 all-gather.6.cloned.1.call-start
  8.0 1.2 convert_reduce_fusion
  9.2 69.6 %all-gather.4.cloned.1.call-done = bf16[2048,512]{1,0:T(8,128)(2,1)} async-done(((bf16[64,512]{1,0:T(8,128)(2,1)}), bf16[2048,512]{1,0:T(8,128)(2,1)}) %all-gather.4.cloned.1.call-update) | async-done | bytes 2097168 | tf_op jit(solution)/shard_map/all_gather | solution.py:28
  78.8 0.0 copy-done
  78.8 2.9 fusion.13
  81.6 53.6 %all-reduce.1 = (f32[512]{0:T(512)S(1)}, f32[512]{0:T(512)S(1)}, f32[512]{0:T(512)S(1)}, f32[512]{0:T(512)S(1)}) all-reduce(f32[512]{0:T(512)S(1)} %get-tuple-element.11, f32[512]{0:T(512)S(1)} %get-tuple-element.10, f32[512]{0:T(512)S(1)} %get-tuple-element.9, f32[512]{0:T(512)S(1)} %get-tuple-element.8), channel_id=1, replica_groups=mesh['dp'=32,'feat'=8] {'dp'}, use_global_device_ids=true, to_apply=%region_7.0 | all-reduce | flops 2048 | bytes 16384 | tf_op jit(solution)/shard_map/psum | solution.py:33
  135.2 2.0 fusion.1
  137.2 0.0 all-gather.6.cloned.1.call-update
  137.2 0.0 reduce-scatter.5.cloned.1.call-start
  137.3 76.2 %all-gather.6.cloned.1.call-done = bf16[512,4096]{1,0:T(8,128)(2,1)} async-done(((bf16[512,512]{1,0:T(8,128)(2,1)}), bf16[512,4096]{1,0:T(8,128)(2,1)}) %all-gather.6.cloned.1.call-update) | async-done | bytes 4194320 | tf_op jit(solution)/shard_map/all_gather | solution.py:37
  213.4 7.8 %fusion.4 = f32[512,4096]{1,0:T(8,128)} fusion(bf16[512,4096]{1,0:T(8,128)(2,1)} %all-gather.6.cloned.1.call-done, f32[512,512]{1,0:T(8,128)S(1)} %get-tuple-element.24, f32[512]{0:T(512)S(1)} %get-tuple-element.21, f32[512]{0:T(512)S(1)} %get-tuple-element.20), kind=kOutput, calls=%fused_computation.13 | convolution fusion | flops 2148270080 | bytes 13635584 | tf_op jit(solution)/shard_map/dot_general | solution.py:41
  221.2 0.0 reduce-scatter.5.cloned.1.call-update
  221.3 0.0 all-gather.8.cloned.1.call-start
  221.3 123.7 %reduce-scatter.5.cloned.1.call-done = f32[16,4096]{1,0:T(8,128)} async-done(((f32[512,4096]{1,0:T(8,128)}), f32[16,4096]{1,0:T(8,128)}) %reduce-scatter.5.cloned.1.call-update) | async-done | bytes 262160 | tf_op jit(solution)/shard_map/reduce_scatter | solution.py:44
  345.1 2.3 select_convert_fusion
  347.4 0.0 all-gather.8.cloned.1.call-update
  347.4 0.0 reduce-scatter.7.cloned.1.call-start
  347.5 67.1 %all-gather.8.cloned.1.call-done = bf16[512,4096]{1,0:T(8,128)(2,1)} async-done(((bf16[16,4096]{1,0:T(8,128)(2,1)}), bf16[512,4096]{1,0:T(8,128)(2,1)}) %all-gather.8.cloned.1.call-update) | async-done | bytes 4194320 | tf_op jit(solution)/shard_map/all_gather | solution.py:58
  414.6 6.8 %fusion.12 = (f32[512]{0:T(512)S(1)}, f32[512]{0:T(512)S(1)}, f32[512,512]{1,0:T(8,128)}) fusion(f32[512]{0:T(512)S(1)} %get-tuple-element.21, f32[512,512]{1,0:T(8,128)S(1)} %get-tuple-element.24, f32[512]{0:T(512)S(1)} %get-tuple-element.20, bf16[512,4096]{1,0:T(8,128)(2,1)} %all-gather.6.cloned.1.call-done, ...), kind=kOutput, calls=%fused_computation.31 | convolution fusion | flops 2149055488 | bytes 10493952 | tf_op jit(solution)/shard_map/dot_general | solution.py:56
  421.5 52.6 %all-reduce = (f32[512]{0:T(512)S(1)}, f32[512]{0:T(512)S(1)}) all-reduce(f32[512]{0:T(512)S(1)} %get-tuple-element.7, f32[512]{0:T(512)S(1)} %get-tuple-element.6), channel_id=1, replica_groups=mesh['dp'=32,'feat'=8] {'dp'}, use_global_device_ids=true, to_apply=%region_14.15 | all-reduce | flops 1024 | bytes 8192 | tf_op jit(solution)/shard_map/psum | solution.py:63
  474.1 4.5 convolution_bitcast_fusion
  478.6 5.3 copy.7
  483.9 0.0 reduce-scatter.7.cloned.1.call-update
  483.9 76.1 %psum.53 = f32[]{:T(128)} all-reduce(f32[]{:T(128)} %get-tuple-element.19), channel_id=1, replica_groups=mesh['dp'=32,'feat'=8] {'dp','feat'}, use_global_device_ids=true, to_apply=%region_10.11 | all-reduce | flops 1 | bytes 8 | tf_op jit(solution)/shard_map/psum | solution.py:55
  560.7 39.6 %reduce-scatter.7.cloned.1.call-done = f32[64,512]{1,0:T(8,128)} async-done(((f32[2048,512]{1,0:T(8,128)}), f32[64,512]{1,0:T(8,128)}) %reduce-scatter.7.cloned.1.call-update) | async-done | bytes 131088
  600.3 1.0 copy.8
  601.3 0.8 copy.6
  (5 shorter events, 0.0 us)
Async XLA Ops:
  7.2 71.6 %copy-start = (bf16[512,2048]{1,0:T(8,128)(2,1)S(1)}, bf16[512,2048]{1,0:T(8,128)(2,1)}, u32[]{:S(2)}) copy-start(bf16[512,2048]{1,0:T(8,128)(2,1)} %param.3) | copy-start | bytes 6291460
  7.2 71.6 %all-gather.4.cloned.1.call-start = ((), (), s32[]{:S(2)}) async-start(), calls=%async_computation.2 | async-start | bytes 2162688 | tf_op jit(solution)/shard_map/all_gather | solution.py:28
  7.9 205.5 %all-gather.6.cloned.1.call-start = ((), (), s32[]{:S(2)}) async-start(), calls=%async_computation.3 | async-start | bytes 4718592 | tf_op jit(solution)/shard_map/all_gather | solution.py:37
  137.2 207.8 %reduce-scatter.5.cloned.1.call-start = ((), (), s32[]{:S(2)}) async-start(), calls=%async_computation.4 | async-start | bytes 8650752 | tf_op jit(solution)/shard_map/reduce_scatter | solution.py:44
  221.3 193.3 %all-gather.8.cloned.1.call-start = ((), (), s32[]{:S(2)}) async-start(), calls=%async_computation.5 | async-start | bytes 4325376 | tf_op jit(solution)/shard_map/all_gather | solution.py:58
  347.4 252.9 %reduce-scatter.7.cloned.1.call-start = ((), (), s32[]{:S(2)}) async-start(), calls=%async_computation.6 | async-start | bytes 4325376
Sparse Core Ops, SparseCore 0:
  9.9 68.8 all-gather.3
  137.3 76.0 all-gather.5
  221.4 123.6 reduce-scatter.4
  347.5 67.0 all-gather.7
  484.1 116.1 reduce-scatter.6
where the time goes:
time: 613 us; the launch traced here: 610 us
  waiting for transfers between devices  377 us (62%)
  blocking collectives  182 us (30%)
  matrix products  22 us (4%)
  between operations  15.6 us (3%)
  local copies, waits for them, and re-layouts  7.15 us (1%)
    reduce_scatter x1, waiting for transfers between devices, shards(): lax.psum_scatter(local_corr, 'dp', scatter_dimension=0, tiled=True)  124 us
    all_gather x1, waiting for transfers between devices, shards(): lax.all_gather(teacher_part.astype(jnp.bfloat16), 'feat', axis=1, tiled=T...  76.2 us
    psum x1, blocking collectives, shards(): loss = lax.psum(loss_part, ('dp', 'feat')) / width_all  76.1 us
    all_gather x1, waiting for transfers between devices, shards(): lax.all_gather(weight, 'dp', axis=0, tiled=True)  69.6 us
    all_gather x1, waiting for transfers between devices, shards(): lax.all_gather(slope, 'dp', axis=0, tiled=True)  67.1 us
    psum x1, blocking collectives, shards(): lax.psum((jnp.sum(teacher_float, axis=0), jnp.sum(teacher_float * teacher...  53.6 us
    psum x1, blocking collectives, shards(): lax.psum((jnp.sum(upstream, axis=0), jnp.sum(upstream * student_float, ax...  52.6 us
    unnamed x6, waiting for transfers between devices  40.3 us
  transfers between devices with their start and end apart: 5, of which 5 were waited for; matrix products, arithmetic and copies ran while one was open for 0% of the time, Pallas kernels for 0%

commit v1 on v0

v1 whole, which is shorter than its diff:
```python
import functools

import jax
import jax.numpy as jnp
from jax import lax
from jax.experimental import pallas as pl
from jax.experimental.pallas import tpu as pltpu
from jax.sharding import PartitionSpec as P

OFF_WEIGHT = 0.5
NORM_EPS = 1e-05
LOSS_SCALE = 128.0
F32 = jnp.float32
BF16 = jnp.bfloat16
MESH = pl.DeviceIdType.MESH


def arms(n):
    return ((n // 2, n // 2 - 1), (n // 2 - 1, n // 2))


def around(at, n):
    return lax.rem(at + n, n)


def kernel(
    nz, ny, x_ref, w_ref, t_ref, loss_ref, g_ref,
    tb, tn, xp, wb, pj, sT, cc, cb, xs, xr, sl, uu, gg, gb, gxs, gxr, gcs, gcr,
    ar_t, ar_p, ar_u, tst, lacc, lf, lc,
    tc_s, tc_r, tx_s, tx_r, ty_s, ty_r, xc_s, xc_r, wc_s, wc_r, wx_s, wx_r, wz_s, wz_r,
    cz_s, cz_r, cx_s, cx_r, sx_s, sx_r, sz_s, sz_r, gz_s, gz_r, gx_s, gx_r, gc_s, gc_r,
    at_s, at_r, ap_s, ap_r, au_s, au_r, ts_s, ts_r, lf_s, lf_r, lc_s, lc_r,
):
    d = lax.axis_index("dp")
    f = lax.axis_index("feat")
    chips = 2 * nz
    feats = 2 * ny
    core = lax.rem(d, 2)
    chip = lax.div(d, 2)
    z = lax.rem(chip, nz)
    xl = lax.div(chip, nz)
    y = lax.rem(f, ny)
    xh = lax.div(f, ny)
    rows = x_ref.shape[0]
    cols = w_ref.shape[1]
    half = cols // 2
    total_rows = float(rows * 2 * chips)
    width_all = cols * feats

    mate = (d + 1 - 2 * core, f)

    def dp_at(chip_at):
        return (chip_at * 2 + core, f)

    def z_at(at):
        return dp_at(xl * nz + at)

    def y_at(at):
        return (d, xh * ny + at)

    x_mate = dp_at((1 - xl) * nz + z)
    h_mate = (d, (1 - xh) * ny + y)

    sent = []

    def copy(src, dst, s, r, to):
        return pltpu.make_async_remote_copy(
            src_ref=src, dst_ref=dst, send_sem=s, recv_sem=r, device_id=to, device_id_type=MESH
        )

    def send(src, dst, s, r, to):
        c = copy(src, dst, s, r, to)
        c.start()
        sent.append(c)

    def arrived(dst, s, r, to):
        copy(dst, dst, s, r, to).wait_recv()

    def ag_step(s, n, pos, at, slot, ss, rs, streams=(0, 1)):
        for st in streams:
            for dr in (0, 1):
                if s < arms(n)[st][dr]:
                    sgn = 1 - 2 * dr
                    p = around(pos - sgn * s, n)
                    if s > 0:
                        arrived(slot(st, p), ss.at[st, dr, s - 1], rs.at[st, dr, s - 1], mate)
                    send(
                        slot(st, p), slot(st, p), ss.at[st, dr, s], rs.at[st, dr, s],
                        at(around(pos + sgn, n)),
                    )

    def ag_end(n, pos, slot, ss, rs, streams=(0, 1)):
        for st in streams:
            for dr in (0, 1):
                h = arms(n)[st][dr]
                if h:
                    p = around(pos - (1 - 2 * dr) * h, n)
                    arrived(slot(st, p), ss.at[st, dr, h - 1], rs.at[st, dr, h - 1], mate)

    def rs_step(s, n, pos, at, buf, local, ss, rs):
        for st in (1, 0):
            for dr in (0, 1):
                h = arms(n)[st][dr]
                if s < h:
                    sgn = 1 - 2 * dr
                    p = around(pos + sgn * (h - s), n)
                    v = local(st, p)
                    if s > 0:
                        arrived(buf.at[st, dr, s], ss.at[st, dr, s - 1], rs.at[st, dr, s - 1], mate)
                        v = v + buf[st, dr, s].astype(F32)
                    buf[st, dr, s] = v.astype(buf.dtype)
                    send(
                        buf.at[st, dr, s], buf.at[st, dr, s + 1], ss.at[st, dr, s], rs.at[st, dr, s],
                        at(around(pos + sgn, n)),
                    )

    def rs_total(st, n, pos, buf, local, ss, rs):
        v = local(st, pos)
        for dr in (0, 1):
            h = arms(n)[st][dr]
            if h:
                arrived(buf.at[st, dr, h], ss.at[st, dr, h - 1], rs.at[st, dr, h - 1], mate)
                v = v + buf[st, dr, h].astype(F32)
        return v

    def ar_copy(buf, ss, rs, k):
        return copy(buf.at[chip], buf.at[chip], ss.at[k - 1], rs.at[k - 1], dp_at(around(chip + k, chips)))

    def ar_start(buf, ss, rs):
        @pl.loop(1, chips)
        def _(k):
            ar_copy(buf, ss, rs, k).start()

    def ar_wait(buf, ss, rs):
        @pl.loop(1, chips)
        def _(k):
            arrived(buf.at[around(chip - k, chips)], ss.at[k - 1], rs.at[k - 1], mate)

        return jnp.sum(buf[...], axis=0)

    def ar_sent(buf, ss, rs):
        @pl.loop(1, chips)
        def _(k):
            ar_copy(buf, ss, rs, k).wait_send()

    def f_copy(buf, ss, rs, k):
        return copy(buf.at[f], buf.at[f], ss.at[k - 1], rs.at[k - 1], (d, around(f + k, feats)))

    def f_start(buf, ss, rs):
        @pl.loop(1, feats)
        def _(k):
            f_copy(buf, ss, rs, k).start()

    def f_wait(buf, ss, rs):
        @pl.loop(1, feats)
        def _(k):
            arrived(buf.at[around(f - k, feats)], ss.at[k - 1], rs.at[k - 1], mate)

    def f_sent(buf, ss, rs):
        @pl.loop(1, feats)
        def _(k):
            f_copy(buf, ss, rs, k).wait_send()

    def norm_of(sums, squares):
        center = sums / total_rows
        spread = squares / total_rows - center * center
        return center, lax.rsqrt(spread + NORM_EPS)

    barrier = pltpu.get_barrier_semaphore()

    def greet(to):
        pl.semaphore_signal(barrier, inc=1, device_id=to, device_id_type=MESH)

    greet(mate)

    @pl.loop(1, feats)
    def _(k):
        greet((d, around(f + k, feats)))

    @pl.loop(1, chips)
    def _(k):
        greet(dp_at(around(chip + k, chips)))

    my_cols = pl.ds(pl.multiple_of(core * half, half), half)
    mate_cols = pl.ds(pl.multiple_of((1 - core) * half, half), half)
    wb[xl, z, core] = w_ref[:, my_cols]
    tb[0, y, 0] = t_ref[...]
    pl.semaphore_wait(barrier, feats + chips - 1)

    send(w_ref.at[:, mate_cols], wb.at[xl, z, core], wc_s, wc_r, mate)
    send(t_ref, tb.at[0, y, 1], tc_s.at[0, 0], tc_r.at[0, 0], mate)

    def t_slot(st, p):
        return tb.at[st, p, 0]

    def t_next(s, streams):
        ag_step(s, ny, y, y_at, t_slot, ty_s, ty_r, streams)

    t_next(0, (0,))
    send(t_ref, tb.at[1, y, 0], tx_s, tx_r, h_mate)
    send(x_ref, xp, xc_s, xc_r, mate)

    comes = []
    for st in (0, 1):
        order = [(0, None)]
        for s in range(ny // 2):
            for dr in (0, 1):
                if s < arms(ny)[st][dr]:
                    order.append((-(1 - 2 * dr) * (s + 1), (dr, s)))
        comes.append(order)

    def t_hand(st, e):
        off, _ = comes[st][e]
        p = around(y + off, ny)
        send(tb.at[st, p, 0], tb.at[st, p, 1], tc_s.at[st, e], tc_r.at[st, e], mate)

    def t_come(st, e):
        off, (dr, s) = comes[st][e]
        arrived(tb.at[st, around(y + off, ny), 0], ty_s.at[st, dr, s], ty_r.at[st, dr, s], mate)

    def t_normal(st, e, wait_mate=True):
        off, _ = comes[st][e]
        p = around(y + off, ny)
        if wait_mate:
            arrived(tb.at[st, p, 1], tc_s.at[st, e], tc_r.at[st, e], mate)
        at = (xh if st == 0 else 1 - xh) * ny + p
        center = tst[at, 0:1, :]
        recip = tst[at, 1:2, :]
        for slot in (0, 1):

            @pl.loop(0, rows // 64)
            def _(i):
                here = pl.multiple_of(i * 64, 64)
                v = tb[st, p, slot, pl.ds(here, 64), :].astype(F32)
                there = pl.multiple_of(slot * rows + i * 64, 64)
                tn[st, p, pl.ds(there, 64), :] = ((v - center) * recip).astype(BF16)

    def w_slot(st, p):
        return wb.at[xl if st == 0 else 1 - xl, p]

    def w_next(s, streams=(0, 1)):
        ag_step(s, nz, z, z_at, w_slot, wz_s, wz_r, streams)

    arrived(wb.at[xl, z, 1 - core], wc_s, wc_r, mate)
    send(wb.at[xl, z], wb.at[xl, z], wx_s, wx_r, x_mate)
    w_next(0, (0,))

    arrived(tb.at[0, y, 1], tc_s.at[0, 0], tc_r.at[0, 0], mate)

    def t_sum(i, carry):
        a, b = carry
        for slot in (0, 1):
            v = tb[0, y, slot, pl.ds(pl.multiple_of(i * 64, 64), 64), :].astype(F32).reshape(8, 8, cols)
            a = a + jnp.sum(v, axis=0)
            b = b + jnp.sum(v * v, axis=0)
        return a, b

    zero = jnp.zeros((8, cols), F32)
    a, b = lax.fori_loop(0, rows // 64, t_sum, (zero, zero))
    ar_t[chip] = zero
    ar_t[chip, 0:1, :] = jnp.sum(a, axis=0, keepdims=True)
    ar_t[chip, 1:2, :] = jnp.sum(b, axis=0, keepdims=True)
    ar_start(ar_t, at_s, at_r)

    arrived(wb.at[1 - xl, z], wx_s, wx_r, mate)
    w_next(0, (1,))
    w_next(1)

    sums = ar_wait(ar_t, at_s, at_r)
    center, recip = norm_of(sums[0:1], sums[1:2])
    tst[f] = zero
    tst[f, 0:1, :] = center
    tst[f, 1:2, :] = recip
    f_start(tst, ts_s, ts_r)

    for s in range(2, nz // 2):
        w_next(s)
    ag_end(nz, z, w_slot, wz_s, wz_r)

    if len(comes[0]) > 1:
        t_come(0, 1)
        if ny > 2:
            ag_step_own = around(y - 1, ny)
            send(
                tb.at[0, ag_step_own, 0], tb.at[0, ag_step_own, 0],
                ty_s.at[0, 0, 1], ty_r.at[0, 0, 1], y_at(around(y + 1, ny)),
            )
        t_hand(0, 1)
    arrived(tb.at[1, y, 0], tx_s, tx_r, mate)
    t_next(0, (1,))
    t_hand(1, 0)

    arrived(xp, xc_s, xc_r, mate)
    wide = wb.shape[0] * wb.shape[1] * wb.shape[2] * wb.shape[3]
    tile = min(256, rows)
    tiles = rows // tile

    def project(ref, base):
        def body(i, carry):
            a, b = carry
            here = pl.multiple_of(i * tile, tile)
            v = jnp.dot(
                ref[pl.ds(here, tile), :], wb[...].reshape(wide, half), preferred_element_type=F32
            )
            pj[pl.ds(pl.multiple_of(base + i * tile, tile), tile), :] = v
            v = v.reshape(tile // 8, 8, half)
            return a + jnp.sum(v, axis=0), b + jnp.sum(v * v, axis=0)

        return body

    narrow = jnp.zeros((8, half), F32)
    carry = lax.fori_loop(0, tiles, project(x_ref, 0), (narrow, narrow))
    a, b = lax.fori_loop(0, tiles, project(xp, rows), carry)
    ar_p[chip] = zero
    ar_p[chip, 0:1, 0:half] = jnp.sum(a, axis=0, keepdims=True)
    ar_p[chip, 0:1, half:cols] = jnp.sum(b, axis=0, keepdims=True)
    ar_start(ar_p, ap_s, ap_r)

    f_wait(tst, ts_s, ts_r)
    t_normal(0, 0, wait_mate=False)
    if len(comes[0]) > 2:
        t_come(0, 2)
        t_hand(0, 2)
    for e in range(1, min(3, len(comes[0]))):
        t_normal(0, e)

    sums = ar_wait(ar_p, ap_s, ap_r)
    p_center, p_recip = norm_of(sums[0:1, 0:half], sums[0:1, half:cols])
    all_tiles = 2 * tiles
    for i in range(all_tiles):
        v = (pj[i * tile:(i + 1) * tile, :] - p_center) * p_recip
        pj[i * tile:(i + 1) * tile, :] = v
        sT[:, i * tile:(i + 1) * tile] = v.T.astype(BF16)

    span = (ny // 2) * cols

    def correlate(g):
        for h in (0, 1):

            @pl.loop(0, ny // 2)
            def _(j):
                v = jnp.dot(sT[...], tn[g, h * (ny // 2) + j], preferred_element_type=F32)
                cc[g, h, :, pl.ds(pl.multiple_of(j * cols, cols), cols)] = v

    piece = half // nz

    def c_local(g):
        def local(st, p):
            h = xl if st == 0 else 1 - xl
            return cc[g, h, pl.ds(pl.multiple_of(p * piece, piece), piece), :]

        return local

    def c_step(g, s):
        rs_step(s, nz, z, z_at, cb.at[g], c_local(g), cz_s.at[g], cz_r.at[g])

    def c_over(g):
        v = rs_total(1, nz, z, cb.at[g], c_local(g), cz_s.at[g], cz_r.at[g])
        xs[g] = v.astype(xs.dtype)
        send(xs.at[g], xr.at[g], cx_s.at[g], cx_r.at[g], x_mate)

    def slope(g):
        v = rs_total(0, nz, z, cb.at[g], c_local(g), cz_s.at[g], cz_r.at[g])
        arrived(xr.at[g], cx_s.at[g], cx_r.at[g], mate)
        share = (v + xr[g].astype(F32)) / total_rows
        student_index = f * cols + core * half + z * piece + lax.broadcasted_iota(jnp.int32, share.shape, 0)
        group = xh if g == 0 else 1 - xh
        teacher_index = (group * 2 + xl) * span + lax.broadcasted_iota(jnp.int32, share.shape, 1)
        on_diag = student_index == teacher_index
        part = jnp.where(on_diag, (1.0 - share) ** 2, OFF_WEIGHT * share * share)
        lacc[g] = jnp.sum(part.reshape(piece // 8, 8, span), axis=0)
        sl[g, xl, z] = jnp.where(on_diag, -2.0 * (1.0 - share), 2.0 * OFF_WEIGHT * share).astype(BF16)
        send(sl.at[g, xl, z], sl.at[g, xl, z], sx_s.at[g], sx_r.at[g], x_mate)

    def s_slot(g):
        return lambda st, p: sl.at[g, xl if st == 0 else 1 - xl, p]

    def s_step(g, s, streams=(0, 1)):
        ag_step(s, nz, z, z_at, s_slot(g), sz_s.at[g], sz_r.at[g], streams)

    def s_end(g):
        ag_end(nz, z, s_slot(g), sz_s.at[g], sz_r.at[g])

    def s_other(g):
        arrived(sl.at[g, 1 - xl, z], sx_s.at[g], sx_r.at[g], mate)
        s_step(g, 0, (1,))

    def upstream(g):
        @pl.loop(0, all_tiles)
        def _(i):
            here = pl.ds(pl.multiple_of(i * tile, tile), tile)
            v = None if g == 0 else uu[here, :]
            for j in range(ny):
                h, k = j // (ny // 2), j % (ny // 2)
                rhs = sl[g, h, :, :, k * cols:(k + 1) * cols].reshape(half, cols)
                w = lax.dot_general(
                    tn[g, j, here, :], rhs, (((1,), (1,)), ((), ())), preferred_element_type=F32
                )
                v = w if v is None else v + w
            uu[here, :] = v

    for e in range(3, len(comes[0])):
        t_come(0, e)
        t_hand(0, e)
        t_normal(0, e)
    correlate(0)
    c_step(0, 0)
    if len(comes[1]) > 2:
        t_come(1, 2)
        p1 = around(y + 1, ny)
        send(
            tb.at[1, p1, 0], tb.at[1, p1, 0], ty_s.at[1, 1, 1], ty_r.at[1, 1, 1],
            y_at(around(y - 1, ny)),
        )
        t_hand(1, 2)
    t_normal(1, 0)
    if len(comes[1]) > 1:
        t_come(1, 1)
        t_hand(1, 1)
    for s in range(1, nz // 2):
        c_step(0, s)
    for e in range(1, min(3, len(comes[1]))):
        t_normal(1, e)
    c_over(0)
    for e in range(3, len(comes[1])):
        t_come(1, e)
        t_hand(1, e)
        t_normal(1, e)
    correlate(1)
    c_step(1, 0)
    slope(0)
    s_step(0, 0, (0,))
    s_other(0)
    for s in range(1, nz // 2):
        c_step(1, s)
        s_step(0, s)
    c_over(1)
    s_end(0)
    upstream(0)
    slope(1)
    s_step(1, 0, (0,))
    s_other(1)
    for s in range(1, nz // 2):
        s_step(1, s)
    s_end(1)
    upstream(1)

    def u_sum(i, carry):
        a, b = carry
        here = pl.ds(pl.multiple_of(i * tile, tile), tile)
        v = uu[here, :] / total_rows
        uu[here, :] = v
        w = v * pj[here, :]
        return (
            a + jnp.sum(v.reshape(tile // 8, 8, half), axis=0),
            b + jnp.sum(w.reshape(tile // 8, 8, half), axis=0),
        )

    a, b = lax.fori_loop(0, all_tiles, u_sum, (narrow, narrow))
    ar_u[chip] = zero
    ar_u[chip, 0:1, 0:half] = jnp.sum(a, axis=0, keepdims=True)
    ar_u[chip, 0:1, half:cols] = jnp.sum(b, axis=0, keepdims=True)
    part = jnp.sum(lacc[0] + lacc[1], axis=0, keepdims=True)
    for k in range(span // cols):
        ar_u[chip, 1:2, :] += part[:, k * cols:(k + 1) * cols]
    ar_start(ar_u, au_s, au_r)
    sums = ar_wait(ar_u, au_s, au_r)
    mean_g = sums[0:1, 0:half] / total_rows
    mean_x = sums[0:1, half:cols] / total_rows
    for i in range(all_tiles):
        v = uu[i * tile:(i + 1) * tile, :]
        v = p_recip * (v - mean_g - pj[i * tile:(i + 1) * tile, :] * mean_x)
        sT[:, i * tile:(i + 1) * tile] = v.T.astype(BF16)

    strip = gg.shape[3]
    pairs = nz // 2
    for h in (0, 1):

        @pl.loop(0, pairs)
        def _(j):
            here = pl.ds(pl.multiple_of(h * nz * strip + j * 2 * strip, 2 * strip), 2 * strip)
            v = jnp.dot(sT[:, 0:rows], x_ref[:, here], preferred_element_type=F32)
            v = v + jnp.dot(sT[:, rows:2 * rows], xp[:, here], preferred_element_type=F32)
            gg[h, 2 * j] = v[:, 0:strip]
            gg[h, 2 * j + 1] = v[:, strip:2 * strip]

    def g_local(st, p):
        return gg[xl if st == 0 else 1 - xl, p]

    rs_step(0, nz, z, z_at, gb, g_local, gz_s, gz_r)

    v = sums[1:2, 0:128]
    for k in range(1, cols // 128):
        v = v + sums[1:2, k * 128:(k + 1) * 128]
    lf[f] = jnp.broadcast_to(v, (8, 128))
    f_start(lf, lf_s, lf_r)

    for s in range(1, nz // 2):
        rs_step(s, nz, z, z_at, gb, g_local, gz_s, gz_r)
    gxs[...] = rs_total(1, nz, z, gb, g_local, gz_s, gz_r).astype(gxs.dtype)
    send(gxs, gxr, gx_s, gx_r, x_mate)
    f_wait(lf, lf_s, lf_r)
    lc[0] = jnp.sum(lf[...], axis=0)
    send(lc.at[0], lc.at[1], lc_s, lc_r, mate)
    v = rs_total(0, nz, z, gb, g_local, gz_s, gz_r)
    arrived(gxr, gx_s, gx_r, mate)
    v = (LOSS_SCALE * (v + gxr[...].astype(F32))).T
    mine = strip // 2
    low, high = v[0:mine], v[mine:strip]
    first = core == 0
    gcs[...] = jnp.where(first, high, low)
    send(gcs, gcr, gc_s, gc_r, mate)
    g_ref[:, my_cols] = jnp.where(first, low, high)
    arrived(lc.at[1], lc_s, lc_r, mate)
    v = jnp.sum(lc[0] + lc[1], axis=1, keepdims=True) / width_all
    loss_ref[...] = jnp.broadcast_to(v, (8, 128))
    arrived(gcr, gc_s, gc_r, mate)
    g_ref[:, mate_cols] = gcr[...]

    for c in sent:
        c.wait_send()
    ar_sent(ar_t, at_s, at_r)
    ar_sent(ar_p, ap_s, ap_r)
    ar_sent(ar_u, au_s, au_r)
    f_sent(tst, ts_s, ts_r)
    f_sent(lf, lf_s, lf_r)


def shards(nz, ny, student, weight, teacher):
    rows, wide = student.shape
    strip_w, cols = weight.shape
    half = cols // 2
    span = (ny // 2) * cols
    chips, feats = 2 * nz, 2 * ny
    steps = nz // 2 + 1
    strip = wide // chips
    piece = half // nz
    V = pltpu.VMEM
    D = pltpu.SemaphoreType.DMA
    data = [
        V((2, ny, 2, rows, cols), BF16),
        V((2, ny, 2 * rows, cols), BF16),
        V((rows, wide), BF16),
        V((2, nz, 2, strip_w, half), BF16),
        V((2 * rows, half), F32),
        V((half, 2 * rows), BF16),
        V((2, 2, half, span), F32),
        V((2, 2, 2, steps, piece, span), BF16),
        V((2, piece, span), BF16),
        V((2, piece, span), BF16),
        V((2, 2, nz, piece, span), BF16),
        V((2 * rows, half), F32),
        V((2, nz, half, strip), F32),
        V((2, 2, steps, half, strip), F32),
        V((half, strip), F32),
        V((half, strip), F32),
        V((strip // 2, half), F32),
        V((strip // 2, half), F32),
        V((chips, 8, cols), F32),
        V((chips, 8, cols), F32),
        V((chips, 8, cols), F32),
        V((feats, 8, cols), F32),
        V((2, 8, span), F32),
        V((feats, 8, 128), F32),
        V((2, 8, 128), F32),
    ]
    sems = []
    for shape in (
        (2, ny), (), (2, 2, ny // 2), (), (), (), (2, 2, nz // 2),
        (2, 2, 2, nz // 2), (2,), (2,), (2, 2, 2, nz // 2), (2, 2, nz // 2), (), (),
        (chips - 1,), (chips - 1,), (chips - 1,), (feats - 1,), (feats - 1,), (),
    ):
        sems += [D(shape), D(shape)]
    vm = pl.BlockSpec(memory_space=pltpu.VMEM)
    loss, grad = pl.pallas_call(
        functools.partial(kernel, nz, ny),
        out_shape=(
            jax.ShapeDtypeStruct((8, 128), F32),
            jax.ShapeDtypeStruct((strip_w, cols), F32),
        ),
        in_specs=[vm] * 3,
        out_specs=(vm, vm),
        scratch_shapes=data + sems,
        compiler_params=pltpu.CompilerParams(
            collective_id=0, has_side_effects=True, vmem_limit_bytes=56 * 1024 * 1024
        ),
    )(student, weight, teacher)
    return loss[0, 0], grad


def solution(mesh):
    placed = (P("dp", None), P("dp", "feat"), P("dp", "feat"))
    nz, ny = mesh.shape["dp"] // 4, mesh.shape["feat"] // 2
    return jax.shard_map(
        functools.partial(shards, nz, ny), mesh=mesh, in_specs=placed,
        out_specs=(P(), P("dp", "feat")), check_vma=False,
    )
```

time: 613 us -> 168 us (0.27)
  waiting for transfers between devices: 377 us -> 0 us
  blocking collectives: 182 us -> 0 us
  Pallas kernels: 0 us -> 165 us
  matrix products: 22 us -> 0 us
  between operations: 15.6 us -> 0.64 us
    all_gather x3 -> x0, waiting for transfers between devices: 213 us -> none  [the longest x1 76.2 us: shards(): lax.all_gather(teacher_part.astype(jnp.bfloat16), 'feat', axis=1, tiled=T...]
    psum x3 -> x0, blocking collectives: 182 us -> none  [the longest x1 76.1 us: shards(): loss = lax.psum(loss_part, ('dp', 'feat')) / width_all]
    pallas_call x0 -> x1, Pallas kernels: none -> 165 us  [shards(): pl.pallas_call(functools.partial(kernel, nz, ny), out_shape=(jax.ShapeDty...]
    reduce_scatter x1 -> x0, waiting for transfers between devices: 124 us -> none  [shards(): lax.psum_scatter(local_corr, 'dp', scatter_dimension=0, tiled=True)]
    unnamed x6 -> x0, waiting for transfers between devices: 40.3 us -> none
    dot_general x4 -> x0, matrix products: 22 us -> none  [the longest x1 7.8 us: shards(): lax.dot_general(student_normal, teacher_normal, (((0,), (0,)), ((), ())),...]
  transfers between devices with their start and end apart: 5 -> 0, of which waited for: 5 -> 0; matrix products, arithmetic and copies ran while one was open for 0% -> 0% of each run, Pallas kernels for 0% -> 0%
where the time goes in v1:
time: 168 us
  Pallas kernels  165 us (98%)
  local copies, waits for them, and re-layouts  2.76 us (2%)
    pallas_call x1, Pallas kernels, shards(): pl.pallas_call(functools.partial(kernel, nz, ny), out_shape=(jax.ShapeDty...  165 us

profile of v1, /device:TPU:1, one launch (start us, length us, event | category | flops | bytes accessed | tf_op | source)
XLA Modules:
  0.0 168.3 jit_solution(8055193691166328317)
XLA Ops:
  0.6 164.9 %shard_map.50 = (f32[8,128]{1,0:T(8,128)}, f32[64,512]{1,0:T(8,128)}) custom-call(bf16[512,2048]{1,0:T(8,128)(2,1)} %x_ref.1, bf16[64,512]{1,0:T(8,128)(2,1)} %w_ref.1, bf16[512,512]{1,0:T(8,128)(2,1)} %t_ref.1), custom_call_target="tpu_custom_call" | custom-call | tf_op jit(solution)/shard_map/pallas_call | solution.py:575
  165.6 1.2 slice.3
  166.8 1.6 copy.6

commit v2 on v0

v2 whole, which is shorter than its diff:
```python
import functools

import jax
import jax.numpy as jnp
from jax import lax
from jax.experimental import pallas as pl
from jax.experimental.pallas import tpu as pltpu
from jax.sharding import PartitionSpec as P

OFF_WEIGHT = 0.5
NORM_EPS = 1e-05
LOSS_SCALE = 128.0
F32 = jnp.float32
BF16 = jnp.bfloat16
MESH = pl.DeviceIdType.MESH


def arms(n):
    return ((n // 2, n // 2 - 1), (n // 2 - 1, n // 2))


def around(at, n):
    return lax.rem(at + n, n)


def kernel(
    nz, ny, x_hbm, w_hbm, t_hbm, loss_ref, g_ref,
    x_ref, tb, tn, rl, xp, wb, pj, sT, cc, ca, cb, xs, xr, bs, br, sl, uu, dT, gg, ga, gb, gxs, gxr, gbr, gcs, gcr,
    ar_t, ar_p, ar_u, tst, lacc, lf, lc,
    out_s, in_s, ar_s, ar_r, tc_r, tx_r, ty_r, xc_r, wc_r, wx_r, wz_r, wy_r,
    ca_r, cx_r, cb_r, bx_r, sx_r, sz_r, sb_r, sy_r, ga_r, gx_r, gb_r, gy_r, gc_r, lc_r,
):
    d = lax.axis_index("dp")
    f = lax.axis_index("feat")
    chips = 2 * nz
    feats = 2 * ny
    core = lax.rem(d, 2)
    chip = lax.div(d, 2)
    z = lax.rem(chip, nz)
    xl = lax.div(chip, nz)
    y = lax.rem(f, ny)
    xh = lax.div(f, ny)
    rows = x_ref.shape[0]
    cols = w_hbm.shape[1]
    half = cols // 2
    total_rows = float(rows * 2 * chips)
    width_all = cols * feats

    mate = (d + 1 - 2 * core, f)

    def dp_at(chip_at):
        return (chip_at * 2 + core, f)

    def z_at(at):
        return dp_at(xl * nz + at)

    def y_at(at):
        return (d, xh * ny + at)

    x_mate = dp_at((1 - xl) * nz + z)
    cross = ((1 - xl) * nz + z) * 2 + core
    x_diag = (cross, (1 - xh) * ny + y)
    x_next = (cross, jnp.where(xl == 0, xh, 1 - xh) * ny + y)
    x_prev = (cross, jnp.where(xl == 0, 1 - xh, xh) * ny + y)

    weigh = {}
    CHIP, WEIGHT, TEACH, CORR, GRAD = range(5)

    def copy(src, dst, s, r, to):
        return pltpu.make_async_remote_copy(
            src_ref=src, dst_ref=dst, send_sem=s, recv_sem=r, device_id=to, device_id_type=MESH
        )

    def send(kind, src, dst, r, to):
        copy(src, dst, out_s.at[kind], r, to).start()
        size = src.dtype.itemsize
        for n in src.shape:
            size *= n
        weigh[kind] = weigh.get(kind, 0) + size

    def arrived(dst, r):
        copy(dst, dst, out_s.at[0], r, mate).wait_recv()

    top = nz // 2

    def hop(k):
        return z_at(around(z + k, nz))

    def ag_go(kind, slot, rs):
        for k, r in ((2, 2), (-2, 3), (1, 0), (-1, 1)):
            send(kind, slot(z), slot(z), rs.at[r], hop(k))

    def ag_on(kind, slot, rs, far=None):
        for dr in (0, 1):
            sgn = 1 - 2 * dr
            block = slot(around(z - 2 * sgn, nz))
            arrived(block, rs.at[2 + dr])
            if far is None:
                side = block.shape[-1] // 2
                part = block.at[:, pl.ds(dr * side, side)]
                send(kind, part, part, rs.at[6 + dr], hop(2 * sgn))
            elif far == dr:
                send(kind, block, block, rs.at[6], hop(2 * sgn))
            send(kind, block, block, rs.at[4 + dr], hop(sgn))

    def ag_near(slot, rs):
        for dr in (0, 1):
            arrived(slot(around(z - 1 + 2 * dr, nz)), rs.at[dr])

    def ag_end(slot, rs, far=None):
        for dr in (0, 1):
            arrived(slot(around(z - 3 + 6 * dr, nz)), rs.at[4 + dr])
        block = slot(around(z + top, nz))
        if far is None:
            side = block.shape[-1] // 2
            for dr in (0, 1):
                arrived(block.at[:, pl.ds(dr * side, side)], rs.at[6 + dr])
        else:
            arrived(block, rs.at[6])

    def agx_to(kind, slot, rs, off):
        block = slot(around(z + off, nz))
        send(kind, block, block, rs.at[off + 3], x_mate)

    def agx_go(kind, slot, rs, xrs):
        ag_go(kind, slot, rs)
        agx_to(kind, slot, xrs, 0)

    def agx_on(kind, slot, rs, xrs):
        ag_on(kind, slot, rs)
        for off in (-2, 2):
            agx_to(kind, slot, xrs, off)
        ag_near(slot, rs)
        for off in (-1, 1):
            agx_to(kind, slot, xrs, off)

    def agx_end(kind, slot, rs, xrs):
        ag_end(slot, rs)
        for off in (-3, 3, top):
            agx_to(kind, slot, xrs, off)

    def agx_last(slot, xrs):
        for off in (0, -2, 2, -1, 1, -3, 3, top):
            arrived(slot(around(z + off, nz)), xrs.at[off + 3])

    def far_step(kind, buf, local, rs):
        for dr in (0, 1):
            buf[dr, 2, dr] = local(dr, around(z + top, nz)).astype(buf.dtype)
            send(kind, buf.at[dr, 2, dr], buf.at[dr, 3, dr], rs.at[dr, 1], hop(2 - 4 * dr))
        for dr in (0, 1):
            sgn = 1 - 2 * dr
            for st in (0, 1):
                buf[dr, 0, st] = local(st, around(z + 3 * sgn, nz)).astype(buf.dtype)
            send(kind, buf.at[dr, 0], buf.at[dr, 1], rs.at[dr, 0], hop(sgn))

    def mid_step(kind, buf, local, rs):
        for dr in (0, 1):
            sgn = 1 - 2 * dr
            arrived(buf.at[dr, 1], rs.at[dr, 0])
            arrived(buf.at[dr, 3, dr], rs.at[dr, 1])
            for st in (0, 1):
                v = local(st, around(z + 2 * sgn, nz)) + buf[dr, 1, st].astype(F32)
                if st == dr:
                    v = v + buf[dr, 3, dr].astype(F32)
                buf[dr, 4, st] = v.astype(buf.dtype)
            send(kind, buf.at[dr, 4], buf.at[dr, 5], rs.at[dr, 2], hop(2 * sgn))

    def near_step(kind, buf, local, rs):
        for dr in (0, 1):
            sgn = 1 - 2 * dr
            for st in (0, 1):
                buf[dr, 6, st] = local(st, around(z + sgn, nz)).astype(buf.dtype)
            send(kind, buf.at[dr, 6], buf.at[dr, 7], rs.at[dr, 3], hop(sgn))

    def sum_end(buf, rs):
        for dr in (0, 1):
            arrived(buf.at[dr, 7], rs.at[dr, 3])
            arrived(buf.at[dr, 5], rs.at[dr, 2])

    def sum_total(st, buf, local):
        v = local(st, z)
        for dr in (0, 1):
            v = v + buf[dr, 5, st].astype(F32) + buf[dr, 7, st].astype(F32)
        return v

    def rs_step(kind, s, buf, local, rs):
        for dr in (0, 1):
            sgn = 1 - 2 * dr
            p = around(z + sgn * (top - s), nz)
            if s == 1:
                arrived(buf.at[dr, s, dr], rs.at[dr, s - 1])
            elif s > 1:
                arrived(buf.at[dr, s], rs.at[dr, s - 1])
            for st in (dr,) if s == 0 else (0, 1):
                v = local(st, p)
                if s > 1 or (s == 1 and st == dr):
                    v = v + buf[dr, s, st].astype(F32)
                buf[dr, s, st] = v.astype(buf.dtype)
            to = z_at(around(z + sgn, nz))
            if s == 0:
                send(kind, buf.at[dr, 0, dr], buf.at[dr, 1, dr], rs.at[dr, 0], to)
            else:
                send(kind, buf.at[dr, s], buf.at[dr, s + 1], rs.at[dr, s], to)

    def rs_end(buf, rs):
        for dr in (0, 1):
            arrived(buf.at[dr, top], rs.at[dr, top - 1])

    def rs_total(st, buf, local):
        return local(st, z) + buf[0, top, st].astype(F32) + buf[1, top, st].astype(F32)

    need = [top, 3, -3, 2, -2, 1, -1, 0]

    def need_at(k):
        return around(z + need[k], nz)

    def x_wait(ks, dst, rs):
        for k in ks:
            arrived(dst.at[need_at(k)], rs.at[k])

    def ar_copy(buf, i, k):
        return copy(buf.at[chip], buf.at[chip], ar_s.at[i], ar_r.at[i], dp_at(around(chip + k, chips)))

    def ar_start(buf, i):
        @pl.loop(1, chips)
        def _(k):
            ar_copy(buf, i, k).start()

    def ar_wait(buf, i):
        arrived(buf.at[pl.ds(0, chips - 1)], ar_r.at[i])
        return jnp.sum(buf[...], axis=0)

    def ar_sent(buf, i, n):
        there = buf.at[pl.ds(0, n - 1)]
        copy(there, there, ar_s.at[i], ar_r.at[i], mate).wait_send()

    def f_start(buf, i):
        @pl.loop(1, feats)
        def _(k):
            copy(buf.at[f], buf.at[f], ar_s.at[i], ar_r.at[i], (d, around(f + k, feats))).start()

    def f_wait(buf, i):
        arrived(buf.at[pl.ds(0, feats - 1)], ar_r.at[i])

    lanes = cols // 128

    def pack(buf, at, row, v):
        for k in range(v.shape[1] // 128):
            buf[at, row + k:row + k + 1, :] = v[:, k * 128:(k + 1) * 128]

    def spread_out(v, row, n):
        return jnp.concatenate([v[row + k:row + k + 1, :] for k in range(n // 128)], axis=1)

    def norm_of(sums, squares):
        center = sums / total_rows
        spread = squares / total_rows - center * center
        return center, lax.rsqrt(spread + NORM_EPS)

    barrier = pltpu.get_barrier_semaphore()

    def greet(to):
        pl.semaphore_signal(barrier, inc=1, device_id=to, device_id_type=MESH)

    greet(mate)
    greet(x_diag)

    @pl.loop(1, feats)
    def _(k):
        greet((d, around(f + k, feats)))

    @pl.loop(1, chips)
    def _(k):
        greet(dp_at(around(chip + k, chips)))

    my_cols = pl.ds(pl.multiple_of(core * half, half), half)
    mate_cols = pl.ds(pl.multiple_of((1 - core) * half, half), half)
    w_in = pltpu.make_async_copy(w_hbm.at[:, my_cols], wb.at[xl, z, core], in_s.at[0])
    t_in = pltpu.make_async_copy(t_hbm, tb.at[0, y, 0], in_s.at[1])
    x_in = pltpu.make_async_copy(x_hbm, x_ref, in_s.at[2])
    w_in.start()
    t_in.start()
    x_in.start()
    pl.semaphore_wait(barrier, feats + chips)

    send(WEIGHT, w_hbm.at[:, mate_cols], wb.at[xl, z, core], wc_r, mate)
    send(TEACH, t_hbm, tb.at[0, y, 1], tc_r.at[0, 0], mate)

    mid = rows // 2
    right, left = y_at(around(y + 1, ny)), y_at(around(y - 1, ny))
    offs = (0, -1, 1, 2)

    def t_at(st, e):
        return tb.at[st, around(y + offs[e], ny), 0]

    def t_hand(st, e):
        send(TEACH, t_at(st, e), tb.at[st, around(y + offs[e], ny), 1], tc_r.at[st, e], mate)

    def t_round(st, src):
        send(TEACH, src, t_at(st, 0), ty_r.at[st, 0, 0], right)
        send(TEACH, src, t_at(st, 0), ty_r.at[st, 1, 0], left)

    def t_pass(st):
        arrived(t_at(st, 1), ty_r.at[st, 0, 0])
        high = t_at(st, 1).at[pl.ds(0, mid)]
        send(TEACH, high, high, ty_r.at[st, 0, 1], right)
        arrived(t_at(st, 2), ty_r.at[st, 1, 0])
        low = t_at(st, 2).at[pl.ds(mid, mid)]
        send(TEACH, low, low, ty_r.at[st, 1, 1], left)
        t_hand(st, 1)
        t_hand(st, 2)

    def t_far(st):
        arrived(t_at(st, 3).at[pl.ds(0, mid)], ty_r.at[st, 0, 1])
        arrived(t_at(st, 3).at[pl.ds(mid, mid)], ty_r.at[st, 1, 1])
        t_hand(st, 3)

    quad = rows // 4
    ways = (x_next, x_prev)

    def t_cross(i):
        for dr in (0, 1):
            part = t_hbm.at[pl.ds((2 * dr + i) * quad, quad)]
            send(TEACH, part, rl.at[dr, i], tx_r.at[dr, i], ways[dr])

    def t_relay(i):
        for dr in (0, 1):
            arrived(rl.at[dr, i], tx_r.at[dr, i])
            there = t_at(1, 0).at[pl.ds((2 * dr + i) * quad, quad)]
            send(TEACH, rl.at[dr, i], there, tx_r.at[dr, 2 + i], ways[dr])

    def t_over():
        for i in (0, 1):
            for dr in (0, 1):
                arrived(t_at(1, 0).at[pl.ds((2 * dr + i) * quad, quad)], tx_r.at[dr, 2 + i])
        t_round(1, t_at(1, 0))
        t_hand(1, 0)

    t_round(0, t_hbm)
    send(CHIP, x_hbm, xp, xc_r, mate)

    def t_normal(st, e, wait_mate=True):
        p = around(y + offs[e], ny)
        if wait_mate:
            arrived(tb.at[st, p, 1], tc_r.at[st, e])
        at = (xh if st == 0 else 1 - xh) * ny + p
        center = spread_out(tst[at], 0, cols)
        recip = spread_out(tst[at], lanes, cols)
        for slot in (0, 1):

            @pl.loop(0, rows // 64)
            def _(i):
                here = pl.multiple_of(i * 64, 64)
                v = tb[st, p, slot, pl.ds(here, 64), :].astype(F32)
                there = pl.multiple_of(slot * rows + i * 64, 64)
                tn[st, p, pl.ds(there, 64), :] = ((v - center) * recip).astype(BF16)

    def w_own(p):
        return wb.at[xl, p, 0]

    def w_other(p):
        return wb.at[1 - xl, p, 0]

    def w_late(p):
        return wb.at[xl, p, 1]

    def w_last(p):
        return wb.at[1 - xl, p, 1]

    w_in.wait()
    arrived(wb.at[xl, z, 1 - core], wc_r)
    send(WEIGHT, w_own(z), w_own(z), wx_r, x_mate)
    ag_go(WEIGHT, w_own, wz_r.at[0])
    agx_go(WEIGHT, w_late, wz_r.at[2], wy_r)

    t_in.wait()
    arrived(tb.at[0, y, 1], tc_r.at[0, 0])

    def t_sum(i, carry):
        a, b = carry
        for slot in (0, 1):
            v = tb[0, y, slot, pl.ds(pl.multiple_of(i * 64, 64), 64), :].astype(F32).reshape(8, 8, cols)
            a = a + jnp.sum(v, axis=0)
            b = b + jnp.sum(v * v, axis=0)
        return a, b

    zero = jnp.zeros((8, cols), F32)
    a, b = lax.fori_loop(0, rows // 64, t_sum, (zero, zero))
    pack(ar_t, chip, 0, jnp.sum(a, axis=0, keepdims=True))
    pack(ar_t, chip, lanes, jnp.sum(b, axis=0, keepdims=True))
    ar_start(ar_t, 0)
    t_cross(0)

    arrived(w_other(z), wx_r)
    ag_go(WEIGHT, w_other, wz_r.at[1])
    ag_on(WEIGHT, w_own, wz_r.at[0], 0)
    agx_on(WEIGHT, w_late, wz_r.at[2], wy_r)
    t_cross(1)
    sums = ar_wait(ar_t, 0)
    center, recip = norm_of(sums[0:lanes], sums[lanes:2 * lanes])
    tst[f, 0:lanes, :] = center
    tst[f, lanes:2 * lanes, :] = recip
    f_start(tst, 4)

    t_relay(0)
    ag_on(WEIGHT, w_other, wz_r.at[1], 1)
    agx_end(WEIGHT, w_late, wz_r.at[2], wy_r)
    t_relay(1)
    t_pass(0)
    ag_near(w_own, wz_r.at[0])
    ag_end(w_own, wz_r.at[0], 0)
    ag_near(w_other, wz_r.at[1])
    ag_end(w_other, wz_r.at[1], 1)
    agx_last(w_last, wy_r)

    x_in.wait()
    arrived(xp, xc_r)
    wide = wb.shape[0] * wb.shape[1] * wb.shape[2] * wb.shape[3]
    tile = min(256, rows)
    tiles = rows // tile

    def project(ref, base):
        def body(i, carry):
            a, b = carry
            here = pl.multiple_of(i * tile, tile)
            v = jnp.dot(
                ref[pl.ds(here, tile), :], wb[...].reshape(wide, half), preferred_element_type=F32
            )
            pj[pl.ds(pl.multiple_of(base + i * tile, tile), tile), :] = v
            v = v.reshape(tile // 8, 8, half)
            return a + jnp.sum(v, axis=0), b + jnp.sum(v * v, axis=0)

        return body

    narrow = jnp.zeros((8, half), F32)
    carry = lax.fori_loop(0, tiles, project(x_ref, 0), (narrow, narrow))
    a, b = lax.fori_loop(0, tiles, project(xp, rows), carry)
    ar_p[chip] = jnp.zeros((8, 128), F32)
    pack(ar_p, chip, 0, jnp.sum(a, axis=0, keepdims=True))
    pack(ar_p, chip, lanes // 2, jnp.sum(b, axis=0, keepdims=True))
    ar_start(ar_p, 1)
    t_far(0)
    t_over()

    f_wait(tst, 4)
    t_normal(0, 0, wait_mate=False)
    t_normal(0, 1)
    t_normal(0, 2)

    sums = ar_wait(ar_p, 1)
    p_center, p_recip = norm_of(spread_out(sums, 0, half), spread_out(sums, lanes // 2, half))
    all_tiles = 2 * tiles
    for i in range(all_tiles):
        v = (pj[i * tile:(i + 1) * tile, :] - p_center) * p_recip
        pj[i * tile:(i + 1) * tile, :] = v
        sT[:, i * tile:(i + 1) * tile] = v.T.astype(BF16)

    span = (ny // 2) * cols

    def correlate(g):
        for h in (0, 1):

            @pl.loop(0, ny // 2)
            def _(j):
                v = jnp.dot(sT[...], tn[g, h * (ny // 2) + j], preferred_element_type=F32)
                cc[g, h, :, pl.ds(pl.multiple_of(j * cols, cols), cols)] = v

    quarter = half // 2
    piece = quarter // nz

    def rows_of(a, p):
        return pl.ds(pl.multiple_of(a * quarter + p * piece, piece), piece)

    side = span // 2

    def sides(st):
        return slice(st * side, (st + 1) * side)

    def ca_local(g):
        return lambda st, p: cc[g, xl if st == 0 else 1 - xl, rows_of(0, p), :]

    def ca_far(g):
        far_step(CORR, ca.at[g], ca_local(g), ca_r.at[g])

    def ca_mid(g):
        mid_step(CORR, ca.at[g], ca_local(g), ca_r.at[g])

    def ca_near(g):
        near_step(CORR, ca.at[g], ca_local(g), ca_r.at[g])

    def ca_over(g):
        sum_end(ca.at[g], ca_r.at[g])
        xs[g] = sum_total(1, ca.at[g], ca_local(g)).astype(xs.dtype)
        send(CORR, xs.at[g], xr.at[g], cx_r.at[g], x_mate)

    def cb_over(a, g):
        bs[g, a] = cc[g, 1 - xl, a * quarter:(a + 1) * quarter, :].astype(BF16).reshape(nz, piece, span)
        for k in range(nz):
            send(CORR, bs.at[g, a, need_at(k)], br.at[g, a, need_at(k)], bx_r.at[g, a, k], x_mate)

    def cb_local(a, g):
        return lambda st, p: cc[g, xl, rows_of(a, p), sides(st)] + br[g, a, p, :, sides(st)].astype(F32)

    def cb_far(a, g):
        x_wait((0, 1, 2), br.at[g, a], bx_r.at[g, a])
        far_step(CORR, cb.at[g, a], cb_local(a, g), cb_r.at[g, a])

    def cb_mid(a, g):
        x_wait((3, 4), br.at[g, a], bx_r.at[g, a])
        mid_step(CORR, cb.at[g, a], cb_local(a, g), cb_r.at[g, a])

    def cb_near(a, g):
        x_wait((5, 6), br.at[g, a], bx_r.at[g, a])
        near_step(CORR, cb.at[g, a], cb_local(a, g), cb_r.at[g, a])

    def slope(a, g):
        if (a, g) == (0, 1):
            v = sum_total(0, ca.at[g], ca_local(g))
            arrived(xr.at[g], cx_r.at[g])
            v = v + xr[g].astype(F32)
        else:
            sum_end(cb.at[g, a], cb_r.at[g, a])
            x_wait((7,), br.at[g, a], bx_r.at[g, a])
            v = jnp.concatenate([sum_total(st, cb.at[g, a], cb_local(a, g)) for st in (0, 1)], axis=1)
        share = v / total_rows
        student_index = (
            f * cols + core * half + a * quarter + z * piece
            + lax.broadcasted_iota(jnp.int32, share.shape, 0)
        )
        group = xh if g == 0 else 1 - xh
        teacher_index = (group * 2 + xl) * span + lax.broadcasted_iota(jnp.int32, share.shape, 1)
        on_diag = student_index == teacher_index
        part = jnp.where(on_diag, (1.0 - share) ** 2, OFF_WEIGHT * share * share)
        lacc[g, a] = jnp.sum(part.reshape(piece // 8, 8, span), axis=0)
        sl[g, xl, a, z] = jnp.where(on_diag, -2.0 * (1.0 - share), 2.0 * OFF_WEIGHT * share).astype(BF16)
        if (a, g) == (0, 1):
            there = sl.at[g, xl, 0, z]
            send(CORR, there, there, sx_r.at[g], x_mate)
            ag_go(CORR, sa_own(g), sz_r.at[g, 0])
        else:
            agx_go(CORR, sb_own(a, g), sb_r.at[g, a], sy_r.at[g, a])

    def sa_own(g):
        return lambda p: sl.at[g, xl, 0, p]

    def sa_mate(g):
        return lambda p: sl.at[g, 1 - xl, 0, p]

    def sb_own(a, g):
        return lambda p: sl.at[g, xl, a, p]

    def sb_mate(a, g):
        return lambda p: sl.at[g, 1 - xl, a, p]

    def sa_other(g):
        arrived(sl.at[g, 1 - xl, 0, z], sx_r.at[g])
        ag_go(CORR, sa_mate(g), sz_r.at[g, 1])

    def sa_on(g):
        ag_on(CORR, sa_own(g), sz_r.at[g, 0], 0)

    def sa_on_other(g):
        ag_on(CORR, sa_mate(g), sz_r.at[g, 1], 1)

    def sa_end(g):
        for st, slot in ((0, sa_own(g)), (1, sa_mate(g))):
            ag_near(slot, sz_r.at[g, st])
            ag_end(slot, sz_r.at[g, st], st)

    def sb_on(a, g):
        agx_on(CORR, sb_own(a, g), sb_r.at[g, a], sy_r.at[g, a])

    def sb_end(a, g):
        agx_end(CORR, sb_own(a, g), sb_r.at[g, a], sy_r.at[g, a])

    def sb_last(a, g):
        agx_last(sb_mate(a, g), sy_r.at[g, a])

    def row_tile(i):
        return pl.ds(pl.multiple_of(i * tile, tile), tile)

    def times_slope(v, g, here, a=None):
        for j in range(ny):
            h, k = j // (ny // 2), j % (ny // 2)
            cut = slice(k * cols, (k + 1) * cols)
            rhs = sl[g, h, :, :, :, cut] if a is None else sl[g, h, a, :, :, cut]
            w = lax.dot_general(
                tn[g, j, here, :], rhs.reshape(half if a is None else quarter, cols),
                (((1,), (1,)), ((), ())), preferred_element_type=F32,
            )
            v = w if v is None else v + w
        return v

    def upstream_first():
        @pl.loop(0, all_tiles)
        def _(i):
            v = times_slope(None, 0, row_tile(i))
            uu[0, row_tile(i), :] = v[:, 0:quarter]
            uu[1, row_tile(i), :] = v[:, quarter:half]

    def upstream_last(a):
        cut = slice(a * quarter, (a + 1) * quarter)

        def body(i, carry):
            here = row_tile(i)
            v = times_slope(uu[a, here, :], 1, here, a) / total_rows
            uu[a, here, :] = v
            w = v * pj[here, cut]
            fold = (tile // 8, 8, quarter)
            return carry[0] + jnp.sum(v.reshape(fold), axis=0), carry[1] + jnp.sum(w.reshape(fold), axis=0)

        none = jnp.zeros((8, quarter), F32)
        b, c = lax.fori_loop(0, all_tiles, body, (none, none))
        ar_u[a, chip] = jnp.zeros((8, 128), F32)
        pack(ar_u.at[a], chip, 0, jnp.sum(b, axis=0, keepdims=True))
        pack(ar_u.at[a], chip, lanes // 4, jnp.sum(c, axis=0, keepdims=True))
        if a == 1:
            part = jnp.sum(lacc[0, 0] + lacc[0, 1] + lacc[1, 0] + lacc[1, 1], axis=0, keepdims=True)
            part = sum(part[:, k * cols:(k + 1) * cols] for k in range(span // cols))
            pack(ar_u.at[a], chip, lanes, part)
        ar_start(ar_u.at[a], 2 + a)

    strip = gg.shape[4]
    pairs = nz // 2

    def gradient(a):
        cut = slice(a * quarter, (a + 1) * quarter)
        sums = ar_wait(ar_u.at[a], 2 + a)
        mean_g = spread_out(sums, 0, quarter) / total_rows
        mean_x = spread_out(sums, lanes // 4, quarter) / total_rows
        for i in range(all_tiles):
            here = slice(i * tile, (i + 1) * tile)
            v = p_recip[:, cut] * (uu[a, here, :] - mean_g - pj[here, cut] * mean_x)
            dT[a, :, here] = v.T.astype(BF16)
        for h in (0, 1):

            @pl.loop(0, pairs)
            def _(j):
                here = pl.ds(pl.multiple_of(h * nz * strip + j * 2 * strip, 2 * strip), 2 * strip)
                v = jnp.dot(dT[a, :, 0:rows], x_ref[:, here], preferred_element_type=F32)
                v = v + jnp.dot(dT[a, :, rows:2 * rows], xp[:, here], preferred_element_type=F32)
                gg[a, h, 2 * j] = v[:, 0:strip]
                gg[a, h, 2 * j + 1] = v[:, strip:2 * strip]

        return sums

    band = quarter // 2

    def ga_local(i):
        return lambda st, p: gg[0, xl if st == 0 else 1 - xl, p, i * band:(i + 1) * band, :]

    def ga_step(s):
        for i in (0, 1):
            rs_step(GRAD, s, ga.at[i], ga_local(i), ga_r.at[i])

    def ga_over():
        for i in (0, 1):
            rs_end(ga.at[i], ga_r.at[i])
            gxs[i] = rs_total(1, ga.at[i], ga_local(i))
            send(GRAD, gxs.at[i], gxr.at[i], gx_r.at[i], x_mate)

    def gb_over():
        for k in range(nz):
            send(GRAD, gg.at[1, 1 - xl, need_at(k)], gbr.at[need_at(k)], gy_r.at[k], x_mate)

    def gb_local(st, p):
        part = slice(st * band, (st + 1) * band)
        return gg[1, xl, p, part, :] + gbr[p, part, :]

    def gb_far():
        x_wait((0, 1, 2), gbr, gy_r)
        far_step(GRAD, gb, gb_local, gb_r)

    def gb_mid():
        x_wait((3, 4), gbr, gy_r)
        mid_step(GRAD, gb, gb_local, gb_r)

    def gb_near():
        x_wait((5, 6), gbr, gy_r)
        near_step(GRAD, gb, gb_local, gb_r)

    mine = strip // 2
    first = core == 0

    def g_core(a):
        if a == 0:
            parts = []
            for i in (0, 1):
                v = rs_total(0, ga.at[i], ga_local(i))
                arrived(gxr.at[i], gx_r.at[i])
                parts.append(v + gxr[i])
            v = jnp.concatenate(parts, axis=0)
        else:
            sum_end(gb, gb_r)
            x_wait((7,), gbr, gy_r)
            v = jnp.concatenate([sum_total(st, gb, gb_local) for st in (0, 1)], axis=0)
        v = (LOSS_SCALE * v).T
        low, high = v[0:mine], v[mine:strip]
        gcs[a] = jnp.where(first, high, low)
        send(GRAD, gcs.at[a], gcr.at[a], gc_r.at[a], mate)
        g_ref[:, pl.ds(pl.multiple_of(core * half + a * quarter, quarter), quarter)] = jnp.where(first, low, high)

    def g_last(a):
        arrived(gcr.at[a], gc_r.at[a])
        g_ref[:, pl.ds(pl.multiple_of((1 - core) * half + a * quarter, quarter), quarter)] = gcr[a]

    t_normal(0, 3)
    correlate(0)
    cb_over(0, 0)
    cb_over(1, 0)
    t_normal(1, 0)
    cb_far(0, 0)
    t_pass(1)
    cb_far(1, 0)
    cb_mid(0, 0)
    cb_near(0, 0)
    t_normal(1, 1)
    t_normal(1, 2)
    cb_mid(1, 0)
    cb_near(1, 0)
    t_far(1)
    slope(0, 0)
    t_normal(1, 3)
    correlate(1)
    ca_far(1)
    cb_over(1, 1)
    ca_near(1)
    slope(1, 0)
    sb_on(0, 0)
    ca_mid(1)
    cb_far(1, 1)
    sb_on(1, 0)
    sb_end(0, 0)
    cb_mid(1, 1)
    cb_near(1, 1)
    ca_over(1)
    sb_end(1, 0)
    slope(0, 1)
    slope(1, 1)
    sb_last(0, 0)
    sb_last(1, 0)
    upstream_first()
    sa_other(1)
    sa_on(1)
    sb_on(1, 1)
    sa_on_other(1)
    sb_end(1, 1)
    sa_end(1)
    upstream_last(0)
    sb_last(1, 1)
    upstream_last(1)
    gradient(0)
    ga_step(0)
    sums = gradient(1)
    gb_over()
    ga_step(1)
    gb_far()
    lf[f] = jnp.broadcast_to(jnp.sum(sums[lanes:2 * lanes], axis=0, keepdims=True), (8, 128))
    f_start(lf, 5)
    ga_step(2)
    gb_mid()
    gb_near()
    ga_step(3)
    f_wait(lf, 5)
    lc[0] = jnp.sum(lf[...], axis=0)
    copy(lc.at[0], lc.at[1], ar_s.at[6], lc_r, mate).start()
    ga_over()
    g_core(1)
    g_core(0)
    arrived(lc.at[1], lc_r)
    loss_ref[0, 0] = jnp.sum((lc[0] + lc[1])[0:1]) / width_all
    g_last(1)
    g_last(0)
    ar_sent(ar_t, 0, chips)
    ar_sent(ar_p, 1, chips)
    ar_sent(ar_u.at[0], 2, chips)
    ar_sent(ar_u.at[1], 3, chips)
    ar_sent(tst, 4, feats)
    ar_sent(lf, 5, feats)
    copy(lc.at[0], lc.at[1], ar_s.at[6], lc_r, mate).wait_send()
    for kind, size in weigh.items():
        there = {WEIGHT: pj, TEACH: tn, CORR: cc}.get(kind, cc.at[0])
        line = there.dtype.itemsize
        for n in there.shape[:-2] + there.shape[-1:]:
            line *= n
        assert size % line == 0 and size // line % 8 == 0
        there = there.at[(slice(None),) * (len(there.shape) - 2) + (pl.ds(0, size // line),)]
        copy(there, there, out_s.at[kind], lc_r, mate).wait_send()


def shards(nz, ny, student, weight, teacher):
    rows, wide = student.shape
    strip_w, cols = weight.shape
    half = cols // 2
    span = (ny // 2) * cols
    chips, feats = 2 * nz, 2 * ny
    steps = nz // 2 + 1
    top = nz // 2
    strip = wide // chips
    quarter = half // 2
    piece = quarter // nz
    V = pltpu.VMEM
    D = pltpu.SemaphoreType.DMA
    data = [
        V((rows, wide), BF16),
        V((2, ny, 2, rows, cols), BF16),
        V((2, ny, 2 * rows, cols), BF16),
        V((2, 2, rows // 4, cols), BF16),
        V((rows, wide), BF16),
        V((2, nz, 2, strip_w, half), BF16),
        V((2 * rows, half), F32),
        V((half, 2 * rows), BF16),
        V((2, 2, half, span), F32),
        V((2, 2, 8, 2, piece, span), BF16),
        V((2, 2, 2, 8, 2, piece, span // 2), BF16),
        V((2, piece, span), BF16),
        V((2, piece, span), BF16),
        V((2, 2, nz, piece, span), BF16),
        V((2, 2, nz, piece, span), BF16),
        V((2, 2, 2, nz, piece, span), BF16),
        V((2, 2 * rows, quarter), F32),
        V((2, quarter, 2 * rows), BF16),
        V((2, 2, nz, quarter, strip), F32),
        V((2, 2, steps, 2, quarter // 2, strip), F32),
        V((2, 8, 2, quarter // 2, strip), F32),
        V((2, quarter // 2, strip), F32),
        V((2, quarter // 2, strip), F32),
        V((nz, quarter, strip), F32),
        V((2, strip // 2, quarter), F32),
        V((2, strip // 2, quarter), F32),
        V((chips, 8, 128), F32),
        V((chips, 8, 128), F32),
        V((2, chips, 8, 128), F32),
        V((feats, 8, 128), F32),
        V((2, 2, 8, span), F32),
        V((feats, 8, 128), F32),
        V((2, 8, 128), F32),
    ]
    sems = [
        D(shape) for shape in (
            (5,), (3,), (7,), (6,),
            (2, ny), (2, 4), (2, 2, 2), (), (), (), (3, nz), (nz,),
            (2, 2, 4), (2,), (2, 2, 2, 4), (2, 2, nz),
            (2,), (2, 2, 7), (2, 2, nz), (2, 2, nz),
            (2, 2, top), (2,), (2, 4), (nz,), (2,), (),
        )
    ]
    vm = pl.BlockSpec(memory_space=pltpu.VMEM)
    sm = pl.BlockSpec(memory_space=pltpu.SMEM)
    far = pl.BlockSpec(memory_space=pl.ANY)
    loss, grad = pl.pallas_call(
        functools.partial(kernel, nz, ny),
        out_shape=(
            jax.ShapeDtypeStruct((1, 1), F32),
            jax.ShapeDtypeStruct((strip_w, cols), F32),
        ),
        in_specs=[far] * 3,
        out_specs=(sm, vm),
        scratch_shapes=data + sems,
        compiler_params=pltpu.CompilerParams(
            collective_id=0, has_side_effects=True, vmem_limit_bytes=56 * 1024 * 1024
        ),
    )(student, weight, teacher)
    return loss.reshape(()), grad


def solution(mesh):
    placed = (P("dp", None), P("dp", "feat"), P("dp", "feat"))
    nz, ny = mesh.shape["dp"] // 4, mesh.shape["feat"] // 2
    return jax.shard_map(
        functools.partial(shards, nz, ny), mesh=mesh, in_specs=placed,
        out_specs=(P(), P("dp", "feat")), check_vma=False,
    )
```

time: 613 us -> 132 us (0.22)
  waiting for transfers between devices: 377 us -> 0 us
  blocking collectives: 182 us -> 0 us
  Pallas kernels: 0 us -> 128 us
  matrix products: 22 us -> 0 us
  between operations: 15.6 us -> 2.45 us
    all_gather x3 -> x0, waiting for transfers between devices: 213 us -> none  [the longest x1 76.2 us: shards(): lax.all_gather(teacher_part.astype(jnp.bfloat16), 'feat', axis=1, tiled=T...]
    psum x3 -> x0, blocking collectives: 182 us -> none  [the longest x1 76.1 us: shards(): loss = lax.psum(loss_part, ('dp', 'feat')) / width_all]
    pallas_call x0 -> x1, Pallas kernels: none -> 128 us  [shards(): pl.pallas_call(functools.partial(kernel, nz, ny), out_shape=(jax.ShapeDty...]
    reduce_scatter x1 -> x0, waiting for transfers between devices: 124 us -> none  [shards(): lax.psum_scatter(local_corr, 'dp', scatter_dimension=0, tiled=True)]
    unnamed x6 -> x0, waiting for transfers between devices: 40.3 us -> none
    dot_general x4 -> x0, matrix products: 22 us -> none  [the longest x1 7.8 us: shards(): lax.dot_general(student_normal, teacher_normal, (((0,), (0,)), ((), ())),...]
  transfers between devices with their start and end apart: 5 -> 0, of which waited for: 5 -> 0; matrix products, arithmetic and copies ran while one was open for 0% -> 0% of each run, Pallas kernels for 0% -> 0%
where the time goes in v2:
time: 132 us
  Pallas kernels  128 us (97%)
  between operations  2.45 us (2%)
  local copies, waits for them, and re-layouts  1.57 us (1%)
    pallas_call x1, Pallas kernels, shards(): pl.pallas_call(functools.partial(kernel, nz, ny), out_shape=(jax.ShapeDty...  128 us

profile of v2, /device:TPU:1, one launch (start us, length us, event | category | flops | bytes accessed | tf_op | source)
XLA Modules:
  0.0 131.9 jit_solution(825698911979722815)
XLA Ops:
  0.6 127.8 %shard_map.50 = (f32[1,1]{1,0:T(1,128)}, f32[64,512]{1,0:T(8,128)}) custom-call(bf16[512,2048]{1,0:T(8,128)(2,1)} %x_hbm.1, bf16[64,512]{1,0:T(8,128)(2,1)} %w_hbm.1, bf16[512,512]{1,0:T(8,128)(2,1)} %t_hbm.1), custom_call_target="tpu_custom_call" | custom-call | tf_op jit(solution)/shard_map/pallas_call | solution.py:850
  129.2 1.6 %copy.8 = f32[64,512]{1,0:T(8,128)} copy(f32[64,512]{1,0:T(8,128)} %get-tuple-element.9) | data formatting | bytes 262144

commit v3 on v2

v3 whole, which is shorter than its diff:
```python
import functools

import jax
import jax.numpy as jnp
from jax import lax
from jax.experimental import pallas as pl
from jax.experimental.pallas import tpu as pltpu
from jax.sharding import PartitionSpec as P

OFF_WEIGHT = 0.5
NORM_EPS = 1e-05
LOSS_SCALE = 128.0
F32 = jnp.float32
BF16 = jnp.bfloat16
MESH = pl.DeviceIdType.MESH


def around(at, n):
    return lax.rem(at + n, n)


def kernel(
    nz, ny, x_hbm, w_hbm, t_hbm, loss_ref, g_ref,
    x_ref, tb, tn, rl, xp, wb, pj, sT, cc, ca, cb, xs, xr, bs, br, sl, uu, gg, gs, gr, ga, gb, gxs, gxr, gcs, gcr,
    ar_t, ar_p, ar_u, ar_n, tst, nst, rowsum, lacc, lf, lc,
    out_s, in_s, ar_s, ar_r, tc_r, tx_r, to_r, ty_r, xc_r, wc_r, wx_r, wz_r, wy_r,
    ca_r, cx_r, cb_r, bx_r, sx_r, sz_r, sb_r, sy_r, ga_r, gx_r, gy_r, gb_r, gc_r, lc_r,
):
    d = lax.axis_index("dp")
    f = lax.axis_index("feat")
    chips = 2 * nz
    feats = 2 * ny
    core = lax.rem(d, 2)
    chip = lax.div(d, 2)
    z = lax.rem(chip, nz)
    xl = lax.div(chip, nz)
    y = lax.rem(f, ny)
    xh = lax.div(f, ny)
    rows = x_ref.shape[0]
    cols = w_hbm.shape[1]
    half = cols // 2
    total_rows = float(rows * 2 * chips)
    width_all = cols * feats

    mate = (d + 1 - 2 * core, f)

    def dp_at(chip_at):
        return (chip_at * 2 + core, f)

    def z_at(at):
        return dp_at(xl * nz + at)

    def y_at(at):
        return (d, xh * ny + at)

    x_mate = dp_at((1 - xl) * nz + z)
    cross = ((1 - xl) * nz + z) * 2 + core
    x_diag = (cross, (1 - xh) * ny + y)
    x_next = (cross, jnp.where(xl == 0, xh, 1 - xh) * ny + y)
    x_prev = (cross, jnp.where(xl == 0, 1 - xh, xh) * ny + y)

    weigh = {}
    CHIP, WEIGHT, TEACH, CROSS, CORR, GRAD = range(6)

    def copy(src, dst, s, r, to):
        return pltpu.make_async_remote_copy(
            src_ref=src, dst_ref=dst, send_sem=s, recv_sem=r, device_id=to, device_id_type=MESH
        )

    def send(kind, src, dst, r, to):
        copy(src, dst, out_s.at[kind], r, to).start()
        size = src.dtype.itemsize
        for n in src.shape:
            size *= n
        weigh[kind] = weigh.get(kind, 0) + size

    def arrived(dst, r):
        copy(dst, dst, out_s.at[0], r, mate).wait_recv()

    top = nz // 2

    def hop(k):
        return z_at(around(z + k, nz))

    def arrived_all(ref, n, r):
        arrived(ref.at[pl.ds(0, n)], r)

    def ag_go(kind, slot, rs):
        for k, r in ((2, 2), (-2, 3), (1, 0), (-1, 0)):
            send(kind, slot(z), slot(z), rs.at[r], hop(k))

    def ag_on(kind, slot, rs, far=None):
        for dr in (0, 1):
            sgn = 1 - 2 * dr
            block = slot(around(z - 2 * sgn, nz))
            arrived(block, rs.at[2 + dr])
            if far is None:
                side = block.shape[-1] // 2
                part = block.at[:, pl.ds(dr * side, side)]
                send(kind, part, part, rs.at[1], hop(2 * sgn))
            elif far == dr:
                send(kind, block, block, rs.at[1], hop(2 * sgn))
            send(kind, block, block, rs.at[1], hop(sgn))

    def ag_end(like, rs):
        arrived_all(like, 2, rs.at[0])
        arrived_all(like, 3, rs.at[1])

    def agx_to(kind, slot, xr, offs):
        for off in offs:
            block = slot(around(z + off, nz))
            send(kind, block, block, xr, x_mate)

    def agx_go(kind, slot, rs, xr):
        ag_go(kind, slot, rs)
        agx_to(kind, slot, xr, (0,))

    def agx_on(kind, slot, rs, xr, like):
        ag_on(kind, slot, rs)
        agx_to(kind, slot, xr, (-2, 2))
        arrived_all(like, 2, rs.at[0])
        agx_to(kind, slot, xr, (-1, 1))

    def agx_end(kind, slot, rs, xr, like):
        arrived_all(like, 3, rs.at[1])
        agx_to(kind, slot, xr, (-3, 3, top))

    def far_step(kind, buf, local, rs):
        for dr in (0, 1):
            buf[dr, 2, 0] = local(dr, around(z + top, nz)).astype(buf.dtype)
            send(kind, buf.at[dr, 2, 0], buf.at[dr, 1, 0], rs.at[dr], hop(2 - 4 * dr))
        for dr in (0, 1):
            sgn = 1 - 2 * dr
            for st in (0, 1):
                buf[dr, 0, st] = local(st, around(z + 3 * sgn, nz)).astype(buf.dtype)
            send(kind, buf.at[dr, 0, pl.ds(0, 2)], buf.at[dr, 1, pl.ds(1, 2)], rs.at[dr], hop(sgn))

    def mid_step(kind, buf, local, rs):
        for dr in (0, 1):
            sgn = 1 - 2 * dr
            arrived(buf.at[dr, 1], rs.at[dr])
            for st in (0, 1):
                v = local(st, around(z + 2 * sgn, nz)) + buf[dr, 1, 1 + st].astype(F32)
                if st == dr:
                    v = v + buf[dr, 1, 0].astype(F32)
                buf[dr, 3, st] = v.astype(buf.dtype)
            send(kind, buf.at[dr, 3, pl.ds(0, 2)], buf.at[dr, 4, pl.ds(0, 2)], rs.at[2], hop(2 * sgn))

    def near_step(kind, buf, local, rs):
        for dr in (0, 1):
            sgn = 1 - 2 * dr
            for st in (0, 1):
                buf[dr, 6, st] = local(st, around(z + sgn, nz)).astype(buf.dtype)
            send(kind, buf.at[dr, 6, pl.ds(0, 2)], buf.at[dr, 5, pl.ds(0, 2)], rs.at[2], hop(sgn))

    def sum_end(buf, rs):
        arrived(buf.at[:, pl.ds(4, 2), pl.ds(0, 2)], rs.at[2])

    def sum_total(st, buf, local):
        v = local(st, z)
        for dr in (0, 1):
            v = v + buf[dr, 4, st].astype(F32) + buf[dr, 5, st].astype(F32)
        return v

    def ring_step(kind, s, buf, local, rs):
        for dr in (0, 1):
            sgn = 1 - 2 * dr
            p = around(z + sgn * (top - s), nz)
            if s == 1:
                arrived(buf.at[dr, s, dr], rs.at[dr, s - 1])
            elif s > 1:
                arrived(buf.at[dr, s], rs.at[dr, s - 1])
            for st in (dr,) if s == 0 else (0, 1):
                v = local(st, p)
                if s > 1 or (s == 1 and st == dr):
                    v = v + buf[dr, s, st]
                buf[dr, s, st] = v
            if s == 0:
                send(kind, buf.at[dr, 0, dr], buf.at[dr, 1, dr], rs.at[dr, 0], hop(sgn))
            else:
                send(kind, buf.at[dr, s], buf.at[dr, s + 1], rs.at[dr, s], hop(sgn))

    def ring_end(buf, rs):
        for dr in (0, 1):
            arrived(buf.at[dr, top], rs.at[dr, top - 1])

    def ring_total(st, buf, local):
        return local(st, z) + buf[0, top, st] + buf[1, top, st]

    need = [top, 3, -3, 2, -2, 1, -1, 0]

    def need_at(k):
        return around(z + need[k], nz)

    def x_group(k):
        return (0, 0, 0, 1, 1, 2, 2, 3)[k]

    def x_wait(i, dst, rs):
        arrived_all(dst, (3, 2, 2, 1)[i], rs.at[i])

    def ar_copy(buf, i, k):
        return copy(buf.at[chip], buf.at[chip], ar_s.at[i], ar_r.at[i], dp_at(around(chip + k, chips)))

    def ar_start(buf, i):
        for k in range(1, chips):
            ar_copy(buf, i, k).start()

    def ar_wait(buf, i):
        arrived(buf.at[pl.ds(0, chips - 1)], ar_r.at[i])
        return jnp.sum(buf[...], axis=0)

    def ar_sent(buf, i, n):
        there = buf.at[pl.ds(0, n - 1)]
        copy(there, there, ar_s.at[i], ar_r.at[i], mate).wait_send()

    def f_start(buf, i):
        @pl.loop(1, feats)
        def _(k):
            copy(buf.at[f], buf.at[f], ar_s.at[i], ar_r.at[i], (d, around(f + k, feats))).start()

    def f_wait(buf, i):
        arrived(buf.at[pl.ds(0, feats - 1)], ar_r.at[i])

    lanes = cols // 128

    def pack(buf, at, row, v):
        for k in range(v.shape[1] // 128):
            buf[at, row + k:row + k + 1, :] = v[:, k * 128:(k + 1) * 128]

    def spread_out(v, row, n):
        return jnp.concatenate([v[row + k:row + k + 1, :] for k in range(n // 128)], axis=1)

    def norm_of(sums, squares):
        center = sums / total_rows
        spread = squares / total_rows - center * center
        return center, lax.rsqrt(spread + NORM_EPS)

    barrier = pltpu.get_barrier_semaphore()

    def greet(to):
        pl.semaphore_signal(barrier, inc=1, device_id=to, device_id_type=MESH)

    greet(mate)
    greet(x_diag)

    @pl.loop(1, feats)
    def _(k):
        greet((d, around(f + k, feats)))

    @pl.loop(1, chips)
    def _(k):
        greet(dp_at(around(chip + k, chips)))

    my_cols = pl.ds(pl.multiple_of(core * half, half), half)
    mate_cols = pl.ds(pl.multiple_of((1 - core) * half, half), half)
    w_in = pltpu.make_async_copy(w_hbm.at[:, my_cols], wb.at[xl, z, core], in_s.at[0])
    t_in = pltpu.make_async_copy(t_hbm, tb.at[0, y, 0], in_s.at[1])
    x_in = pltpu.make_async_copy(x_hbm, x_ref, in_s.at[2])
    w_in.start()
    t_in.start()
    x_in.start()
    rowsum[...] = jnp.zeros_like(rowsum)
    pl.semaphore_wait(barrier, feats + chips)

    send(WEIGHT, w_hbm.at[:, mate_cols], wb.at[xl, z, core], wc_r, mate)
    send(TEACH, t_hbm, tb.at[0, y, 1], tc_r.at[0, 0], mate)

    mid = rows // 2
    right, left = y_at(around(y + 1, ny)), y_at(around(y - 1, ny))
    offs = (0, -1, 1, 2)

    def t_at(st, e):
        return tb.at[st, around(y + offs[e], ny), 0]

    def t_hand(st, e):
        send(TEACH, t_at(st, e), tb.at[st, around(y + offs[e], ny), 1], tc_r.at[st, e], mate)

    def t_round(st, src):
        send(TEACH, src, t_at(st, 0), ty_r.at[st, 0], right)
        send(TEACH, src, t_at(st, 0), ty_r.at[st, 1], left)

    def t_pass(st):
        arrived(t_at(st, 1), ty_r.at[st, 0])
        high = t_at(st, 1).at[pl.ds(0, mid)]
        send(TEACH, high, high, ty_r.at[st, 2], right)
        arrived(t_at(st, 2), ty_r.at[st, 1])
        low = t_at(st, 2).at[pl.ds(mid, mid)]
        send(TEACH, low, low, ty_r.at[st, 2], left)
        t_hand(st, 1)
        t_hand(st, 2)

    def t_far(st):
        arrived(t_at(st, 3), ty_r.at[st, 2])
        t_hand(st, 3)

    quad = rows // 4
    ways = (x_next, x_prev)

    def t_cross(i):
        for dr in (0, 1):
            part = t_hbm.at[pl.ds((2 * dr + i) * quad, quad)]
            send(CROSS, part, rl.at[dr, i], tx_r.at[dr, i], ways[dr])

    def t_relay(i):
        for dr in (0, 1):
            arrived(rl.at[dr, i], tx_r.at[dr, i])
            there = t_at(1, 0).at[pl.ds((2 * dr + i) * quad, quad)]
            send(CROSS, rl.at[dr, i], there, to_r, ways[dr])

    def t_over():
        arrived(t_at(1, 0), to_r)
        t_round(1, t_at(1, 0))
        t_hand(1, 0)

    t_cross(0)
    t_round(0, t_hbm)
    send(CHIP, x_hbm, xp, xc_r, mate)

    def t_normal(st, e, wait_mate=True):
        p = around(y + offs[e], ny)
        if wait_mate:
            arrived(tb.at[st, p, 1], tc_r.at[st, e])
        at = (xh if st == 0 else 1 - xh) * ny + p
        center = spread_out(tst[at], 0, cols)
        recip = spread_out(tst[at], lanes, cols)
        for slot in (0, 1):

            @pl.loop(0, rows // 64)
            def _(i):
                here = pl.multiple_of(i * 64, 64)
                v = tb[st, p, slot, pl.ds(here, 64), :].astype(F32)
                there = pl.multiple_of(slot * rows + i * 64, 64)
                tn[st, p, pl.ds(there, 64), :] = ((v - center) * recip).astype(BF16)

    def w_own(p):
        return wb.at[xl, p, 0]

    def w_other(p):
        return wb.at[1 - xl, p, 0]

    def w_late(p):
        return wb.at[xl, p, 1]

    w_like = wb.at[0, :, 0]

    w_in.wait()
    arrived(wb.at[xl, z, 1 - core], wc_r)
    send(WEIGHT, w_own(z), w_own(z), wx_r, x_mate)
    ag_go(WEIGHT, w_own, wz_r.at[0])
    agx_go(WEIGHT, w_late, wz_r.at[2], wy_r)
    t_cross(1)

    t_in.wait()
    arrived(tb.at[0, y, 1], tc_r.at[0, 0])

    def t_sum(i, carry):
        a, b = carry
        for slot in (0, 1):
            v = tb[0, y, slot, pl.ds(pl.multiple_of(i * 64, 64), 64), :].astype(F32).reshape(8, 8, cols)
            a = a + jnp.sum(v, axis=0)
            b = b + jnp.sum(v * v, axis=0)
        return a, b

    zero = jnp.zeros((8, cols), F32)
    a, b = lax.fori_loop(0, rows // 64, t_sum, (zero, zero))
    pack(ar_t, chip, 0, jnp.sum(a, axis=0, keepdims=True))
    pack(ar_t, chip, lanes, jnp.sum(b, axis=0, keepdims=True))
    ar_start(ar_t, 0)

    arrived(w_other(z), wx_r)
    ag_go(WEIGHT, w_other, wz_r.at[1])
    t_relay(0)
    ag_on(WEIGHT, w_own, wz_r.at[0], 0)
    agx_on(WEIGHT, w_late, wz_r.at[2], wy_r, w_like)
    t_relay(1)
    ag_on(WEIGHT, w_other, wz_r.at[1], 1)
    t_pass(0)
    agx_end(WEIGHT, w_late, wz_r.at[2], wy_r, w_like)
    sums = ar_wait(ar_t, 0)
    center, recip = norm_of(sums[0:lanes], sums[lanes:2 * lanes])
    tst[f, 0:lanes, :] = center
    tst[f, lanes:2 * lanes, :] = recip
    f_start(tst, 3)
    ag_end(w_like, wz_r.at[0])

    x_in.wait()
    arrived(xp, xc_r)
    wide = wb.shape[1] * wb.shape[2] * wb.shape[3]
    tile = min(256, rows)
    tiles = rows // tile
    narrow = jnp.zeros((8, half), F32)

    def project(ref, base, h, last):
        deep = pl.ds(pl.multiple_of(h * wide, wide), wide)

        def body(i, carry):
            here = pl.ds(pl.multiple_of(i * tile, tile), tile)
            there = pl.ds(pl.multiple_of(base + i * tile, tile), tile)
            v = jnp.dot(ref[here, deep], wb[h].reshape(wide, half), preferred_element_type=F32)
            if last:
                v = v + pj[there, :]
            pj[there, :] = v
            if not last:
                return carry
            v = v.reshape(tile // 8, 8, half)
            return carry[0] + jnp.sum(v, axis=0), carry[1] + jnp.sum(v * v, axis=0)

        return body

    lax.fori_loop(0, tiles, project(x_ref, 0, xl, False), 0)
    lax.fori_loop(0, tiles, project(xp, rows, xl, False), 0)
    t_over()
    ag_end(w_like, wz_r.at[1])
    arrived(wb.at[1 - xl, :, 1], wy_r)
    carry = lax.fori_loop(0, tiles, project(x_ref, 0, 1 - xl, True), (narrow, narrow))
    a, b = lax.fori_loop(0, tiles, project(xp, rows, 1 - xl, True), carry)
    ar_p[chip] = jnp.zeros((8, 128), F32)
    pack(ar_p, chip, 0, jnp.sum(a, axis=0, keepdims=True))
    pack(ar_p, chip, lanes // 2, jnp.sum(b, axis=0, keepdims=True))
    ar_start(ar_p, 1)
    t_far(0)
    f_wait(tst, 3)
    t_normal(0, 0, wait_mate=False)

    def n_sum(i, total):
        v = tn[0, y, pl.ds(pl.multiple_of(i * 64, 64), 64), :].astype(F32)
        return total + jnp.sum(v.reshape(8, 8, cols), axis=0)

    n_sums = lax.fori_loop(0, 2 * rows // 64, n_sum, zero)
    ar_n[chip] = jnp.zeros((8, 128), F32)
    pack(ar_n, chip, 0, jnp.sum(n_sums, axis=0, keepdims=True))
    ar_start(ar_n, 5)
    t_normal(0, 1)
    t_normal(0, 2)

    sums = ar_wait(ar_p, 1)
    p_center, p_recip = norm_of(spread_out(sums, 0, half), spread_out(sums, lanes // 2, half))
    all_tiles = 2 * tiles
    for i in range(all_tiles):
        v = (pj[i * tile:(i + 1) * tile, :] - p_center) * p_recip
        pj[i * tile:(i + 1) * tile, :] = v
        sT[:, i * tile:(i + 1) * tile] = v.T.astype(BF16)

    span = (ny // 2) * cols

    def correlate(g, h):
        @pl.loop(0, ny // 2)
        def _(j):
            v = jnp.dot(sT[...], tn[g, h * (ny // 2) + j], preferred_element_type=F32)
            cc[g, h, :, pl.ds(pl.multiple_of(j * cols, cols), cols)] = v

    quarter = half // 2
    piece = quarter // nz

    def rows_of(a, p):
        return pl.ds(pl.multiple_of(a * quarter + p * piece, piece), piece)

    side = span // 2

    def sides(st):
        return slice(st * side, (st + 1) * side)

    def ca_local(g):
        return lambda st, p: cc[g, xl if st == 0 else 1 - xl, rows_of(0, p), :]

    def ca_far(g):
        far_step(CORR, ca.at[g], ca_local(g), ca_r.at[g])

    def ca_mid(g):
        mid_step(CORR, ca.at[g], ca_local(g), ca_r.at[g])

    def ca_near(g):
        near_step(CORR, ca.at[g], ca_local(g), ca_r.at[g])

    def ca_over(g):
        sum_end(ca.at[g], ca_r.at[g])
        xs[g] = sum_total(1, ca.at[g], ca_local(g)).astype(xs.dtype)
        send(CORR, xs.at[g], xr.at[g], cx_r.at[g], x_mate)

    def cb_over(g):
        bs[g] = cc[g, 1 - xl, quarter:half, :].astype(BF16).reshape(nz, piece, span)
        for k in range(nz):
            send(CORR, bs.at[g, need_at(k)], br.at[g, need_at(k)], bx_r.at[g, x_group(k)], x_mate)

    def cb_local(g):
        return lambda st, p: cc[g, xl, rows_of(1, p), sides(st)] + br[g, p, :, sides(st)].astype(F32)

    def cb_far(g):
        x_wait(0, br.at[g], bx_r.at[g])
        far_step(CORR, cb.at[g], cb_local(g), cb_r.at[g])

    def cb_mid(g):
        x_wait(1, br.at[g], bx_r.at[g])
        mid_step(CORR, cb.at[g], cb_local(g), cb_r.at[g])

    def cb_near(g):
        x_wait(2, br.at[g], bx_r.at[g])
        near_step(CORR, cb.at[g], cb_local(g), cb_r.at[g])

    def slope(a, g):
        if a == 0:
            v = sum_total(0, ca.at[g], ca_local(g))
            arrived(xr.at[g], cx_r.at[g])
            v = v + xr[g].astype(F32)
        else:
            sum_end(cb.at[g], cb_r.at[g])
            x_wait(3, br.at[g], bx_r.at[g])
            v = jnp.concatenate([sum_total(st, cb.at[g], cb_local(g)) for st in (0, 1)], axis=1)
        share = v / total_rows
        student_index = (
            f * cols + core * half + a * quarter + z * piece
            + lax.broadcasted_iota(jnp.int32, share.shape, 0)
        )
        group = xh if g == 0 else 1 - xh
        teacher_index = (group * 2 + xl) * span + lax.broadcasted_iota(jnp.int32, share.shape, 1)
        on_diag = student_index == teacher_index
        part = jnp.where(on_diag, (1.0 - share) ** 2, OFF_WEIGHT * share * share)
        lacc[g, a] = jnp.sum(part.reshape(piece // 8, 8, span), axis=0)
        lean = jnp.where(on_diag, -2.0 * (1.0 - share), 2.0 * OFF_WEIGHT * share).astype(BF16)
        sl[g, xl, a, z] = lean
        lean = lean.astype(F32)
        at = group * ny + xl * (ny // 2)
        n_row = jnp.concatenate([spread_out(nst[at + k], 0, cols) for k in range(ny // 2)], axis=1)
        here = pl.ds(pl.multiple_of(z * piece, piece), piece)
        for k, v in ((a, lean * n_row), (2 + a, lean * share)):
            v = jnp.broadcast_to(jnp.sum(v, axis=1, keepdims=True), (piece, 128))
            rowsum[k, here, :] = v if g == 0 else rowsum[k, here, :] + v
        if (a, g) == (0, 1):
            there = sl.at[g, xl, 0, z]
            send(CORR, there, there, sx_r, x_mate)
            ag_go(CORR, sa_own(g), sz_r.at[0])
        else:
            agx_go(CORR, sb_own(a, g), sb_r.at[g, a], sy_r.at[g, a])

    def sa_own(g):
        return lambda p: sl.at[g, xl, 0, p]

    def sa_mate(g):
        return lambda p: sl.at[g, 1 - xl, 0, p]

    def sb_own(a, g):
        return lambda p: sl.at[g, xl, a, p]

    def sa_other(g):
        arrived(sl.at[g, 1 - xl, 0, z], sx_r)
        ag_go(CORR, sa_mate(g), sz_r.at[1])

    def sa_on(g):
        ag_on(CORR, sa_own(g), sz_r.at[0], 0)

    def sa_on_other(g):
        ag_on(CORR, sa_mate(g), sz_r.at[1], 1)

    def sa_end(g):
        ag_end(sl.at[g, 0, 0], sz_r.at[0])
        ag_end(sl.at[g, 0, 0], sz_r.at[1])

    def sb_on(a, g):
        agx_on(CORR, sb_own(a, g), sb_r.at[g, a], sy_r.at[g, a], sl.at[g, xl, a])

    def sb_end(a, g):
        agx_end(CORR, sb_own(a, g), sb_r.at[g, a], sy_r.at[g, a], sl.at[g, xl, a])

    def sb_last(a, g):
        arrived(sl.at[g, 1 - xl, a], sy_r.at[g, a])

    def row_tile(i):
        return pl.ds(pl.multiple_of(i * tile, tile), tile)

    def times_slope(v, g, here):
        for j in range(ny):
            h, k = j // (ny // 2), j % (ny // 2)
            rhs = sl[g, h, :, :, :, k * cols:(k + 1) * cols].reshape(half, cols)
            w = lax.dot_general(
                tn[g, j, here, :], rhs, (((1,), (1,)), ((), ())), preferred_element_type=F32
            )
            v = w if v is None else v + w
        return v

    def upstream_first():
        @pl.loop(0, all_tiles)
        def _(i):
            uu[row_tile(i), :] = times_slope(None, 0, row_tile(i))

    def u_start():
        for k in range(4):
            ar_u[chip, k:k + 1, :] = rowsum[k].T[0:1]
        part = jnp.sum(lacc[0, 0] + lacc[0, 1] + lacc[1, 0] + lacc[1, 1], axis=0, keepdims=True)
        part = sum(part[:, k * cols:(k + 1) * cols] for k in range(span // cols))
        pack(ar_u, chip, lanes, part)
        ar_start(ar_u, 2)

    def delta():
        sums = ar_wait(ar_u, 2)
        mean_g = spread_out(sums, 0, half) / (total_rows * total_rows)
        mean_x = spread_out(sums, lanes // 2, half) / total_rows

        @pl.loop(0, all_tiles)
        def _(i):
            here = row_tile(i)
            v = times_slope(uu[here, :], 1, here) / total_rows
            v = p_recip * (v - mean_g - pj[here, :] * mean_x)
            sT[:, pl.ds(pl.multiple_of(i * tile, tile), tile)] = v.T.astype(BF16)

        return sums

    strip = gg.shape[3]
    band = quarter // 2

    def gradient(h, out):
        @pl.loop(0, nz // 2)
        def _(j):
            here = pl.ds(pl.multiple_of(h * nz * strip + j * 2 * strip, 2 * strip), 2 * strip)
            v = jnp.dot(sT[:, 0:rows], x_ref[:, here], preferred_element_type=F32)
            v = v + jnp.dot(sT[:, rows:2 * rows], xp[:, here], preferred_element_type=F32)
            v = v.astype(out.dtype)
            for a in (0, 1):
                for k in (0, 1):
                    out[a, 2 * j + k] = v[a * quarter:(a + 1) * quarter, k * strip:(k + 1) * strip]

    def ga_local(i):
        part = slice(i * band, (i + 1) * band)
        return lambda st, p: (gg if st == 0 else gs)[0, p, part, :]

    def ga_step(s):
        for i in (0, 1):
            ring_step(GRAD, s, ga.at[i], ga_local(i), ga_r.at[i])

    def ga_over():
        for i in (0, 1):
            ring_end(ga.at[i], ga_r.at[i])
            gxs[i] = ring_total(1, ga.at[i], ga_local(i))
            send(GRAD, gxs.at[i], gxr.at[i], gx_r.at[i], x_mate)

    def gb_over():
        for k in range(nz):
            send(GRAD, gs.at[1, need_at(k)], gr.at[need_at(k)], gy_r.at[x_group(k)], x_mate)

    def gb_local(st, p):
        part = slice(st * band, (st + 1) * band)
        return gg[1, p, part, :] + gr[p, part, :]

    def gb_far():
        x_wait(0, gr, gy_r)
        far_step(GRAD, gb, gb_local, gb_r)

    def gb_mid():
        x_wait(1, gr, gy_r)
        mid_step(GRAD, gb, gb_local, gb_r)

    def gb_near():
        x_wait(2, gr, gy_r)
        near_step(GRAD, gb, gb_local, gb_r)

    mine = strip // 2
    first = core == 0

    def g_core(a):
        if a == 0:
            parts = []
            for i in (0, 1):
                v = ring_total(0, ga.at[i], ga_local(i))
                arrived(gxr.at[i], gx_r.at[i])
                parts.append(v + gxr[i])
        else:
            sum_end(gb, gb_r)
            x_wait(3, gr, gy_r)
            parts = [sum_total(st, gb, gb_local) for st in (0, 1)]
        v = jnp.concatenate(parts, axis=0)
        v = (LOSS_SCALE * v).T
        low, high = v[0:mine], v[mine:strip]
        gcs[a] = jnp.where(first, high, low)
        send(GRAD, gcs.at[a], gcr.at[a], gc_r.at[a], mate)
        g_ref[:, pl.ds(pl.multiple_of(core * half + a * quarter, quarter), quarter)] = jnp.where(first, low, high)

    def g_last(a):
        arrived(gcr.at[a], gc_r.at[a])
        g_ref[:, pl.ds(pl.multiple_of((1 - core) * half + a * quarter, quarter), quarter)] = gcr[a]

    t_normal(0, 3)
    correlate(0, 1 - xl)
    cb_over(0)
    correlate(0, xl)
    ca_far(0)
    ca_near(0)
    t_normal(1, 0)
    nst[f] = ar_wait(ar_n, 5)
    f_start(nst, 6)
    cb_far(0)
    ca_mid(0)
    t_pass(1)
    cb_mid(0)
    cb_near(0)
    ca_over(0)
    t_normal(1, 1)
    t_normal(1, 2)
    t_far(1)
    f_wait(nst, 6)
    slope(1, 0)
    slope(0, 0)
    t_normal(1, 3)
    correlate(1, 1 - xl)
    cb_over(1)
    correlate(1, xl)
    ca_far(1)
    ca_near(1)
    cb_far(1)
    ca_mid(1)
    sb_on(0, 0)
    sb_on(1, 0)
    cb_mid(1)
    cb_near(1)
    ca_over(1)
    sb_end(0, 0)
    sb_end(1, 0)
    slope(0, 1)
    slope(1, 1)
    u_start()
    sa_other(1)
    sa_on(1)
    sb_on(1, 1)
    sa_on_other(1)
    sb_last(0, 0)
    sb_last(1, 0)
    upstream_first()
    sb_end(1, 1)
    sa_end(1)
    sb_last(1, 1)
    sums = delta()
    gradient(1 - xl, gs)
    gb_over()
    gradient(xl, gg)
    ga_step(0)
    lf[f] = jnp.broadcast_to(jnp.sum(sums[lanes:2 * lanes], axis=0, keepdims=True), (8, 128))
    f_start(lf, 4)
    ga_step(1)
    gb_far()
    ga_step(2)
    gb_mid()
    ga_step(3)
    gb_near()
    f_wait(lf, 4)
    lc[0] = jnp.sum(lf[...], axis=0)
    copy(lc.at[0], lc.at[1], ar_s.at[7], lc_r, mate).start()
    ga_over()
    g_core(1)
    g_core(0)
    arrived(lc.at[1], lc_r)
    loss_ref[0, 0] = jnp.sum((lc[0] + lc[1])[0:1]) / width_all
    g_last(1)
    g_last(0)
    ar_sent(ar_t, 0, chips)
    ar_sent(ar_p, 1, chips)
    ar_sent(ar_u, 2, chips)
    ar_sent(ar_n, 5, chips)
    ar_sent(nst, 6, feats)
    ar_sent(tst, 3, feats)
    ar_sent(lf, 4, feats)
    copy(lc.at[0], lc.at[1], ar_s.at[7], lc_r, mate).wait_send()
    for kind, size in weigh.items():
        there = {WEIGHT: pj, TEACH: tn, CORR: cc}.get(kind, cc.at[0])
        line = there.dtype.itemsize
        for n in there.shape[:-2] + there.shape[-1:]:
            line *= n
        assert size % line == 0 and size // line % 8 == 0
        there = there.at[(slice(None),) * (len(there.shape) - 2) + (pl.ds(0, size // line),)]
        copy(there, there, out_s.at[kind], lc_r, mate).wait_send()


def shards(nz, ny, student, weight, teacher):
    rows, wide = student.shape
    strip_w, cols = weight.shape
    half = cols // 2
    span = (ny // 2) * cols
    chips, feats = 2 * nz, 2 * ny
    strip = wide // chips
    quarter = half // 2
    piece = quarter // nz
    V = pltpu.VMEM
    D = pltpu.SemaphoreType.DMA
    data = [
        V((rows, wide), BF16),
        V((2, ny, 2, rows, cols), BF16),
        V((2, ny, 2 * rows, cols), BF16),
        V((2, 2, rows // 4, cols), BF16),
        V((rows, wide), BF16),
        V((2, nz, 2, strip_w, half), BF16),
        V((2 * rows, half), F32),
        V((half, 2 * rows), BF16),
        V((2, 2, half, span), F32),
        V((2, 2, 7, 3, piece, span), BF16),
        V((2, 2, 7, 3, piece, span // 2), BF16),
        V((2, piece, span), BF16),
        V((2, piece, span), BF16),
        V((2, nz, piece, span), BF16),
        V((2, nz, piece, span), BF16),
        V((2, 2, 2, nz, piece, span), BF16),
        V((2 * rows, half), F32),
        V((2, nz, quarter, strip), F32),
        V((2, nz, quarter, strip), F32),
        V((nz, quarter, strip), F32),
        V((2, 2, nz // 2 + 1, 2, quarter // 2, strip), F32),
        V((2, 7, 3, quarter // 2, strip), F32),
        V((2, quarter // 2, strip), F32),
        V((2, quarter // 2, strip), F32),
        V((2, strip // 2, quarter), F32),
        V((2, strip // 2, quarter), F32),
        V((chips, 8, 128), F32),
        V((chips, 8, 128), F32),
        V((chips, 8, 128), F32),
        V((chips, 8, 128), F32),
        V((feats, 8, 128), F32),
        V((feats, 8, 128), F32),
        V((4, 128, 128), F32),
        V((2, 2, 8, span), F32),
        V((feats, 8, 128), F32),
        V((2, 8, 128), F32),
    ]
    sems = [
        D(shape) for shape in (
            (6,), (3,), (8,), (7,),
            (2, ny), (2, 2), (), (2, 3), (), (), (), (3, 4), (),
            (2, 3), (2,), (2, 3), (2, 4),
            (), (2, 4), (2, 2, 4), (2, 2),
            (2, 2, nz // 2), (2,), (4,), (3,), (2,), (),
        )
    ]
    vm = pl.BlockSpec(memory_space=pltpu.VMEM)
    sm = pl.BlockSpec(memory_space=pltpu.SMEM)
    far = pl.BlockSpec(memory_space=pl.ANY)
    loss, grad = pl.pallas_call(
        functools.partial(kernel, nz, ny),
        out_shape=(
            jax.ShapeDtypeStruct((1, 1), F32),
            jax.ShapeDtypeStruct((strip_w, cols), F32),
        ),
        in_specs=[far] * 3,
        out_specs=(sm, vm),
        scratch_shapes=data + sems,
        compiler_params=pltpu.CompilerParams(
            collective_id=0, has_side_effects=True, vmem_limit_bytes=56 * 1024 * 1024
        ),
    )(student, weight, teacher)
    return loss.reshape(()), grad


def solution(mesh):
    placed = (P("dp", None), P("dp", "feat"), P("dp", "feat"))
    nz, ny = mesh.shape["dp"] // 4, mesh.shape["feat"] // 2
    return jax.shard_map(
        functools.partial(shards, nz, ny), mesh=mesh, in_specs=placed,
        out_specs=(P(), P("dp", "feat")), check_vma=False,
    )
```

time: 132 us -> 121 us (0.917)
  Pallas kernels: 128 us -> 117 us
    pallas_call x1, Pallas kernels: 128 us -> 117 us  [shards(): pl.pallas_call(functools.partial(kernel, nz, ny), out_shape=(jax.ShapeDty...]
where the time goes in v3:
time: 121 us
  Pallas kernels  117 us (97%)
  between operations  2.45 us (2%)
  local copies, waits for them, and re-layouts  1.57 us (1%)
    pallas_call x1, Pallas kernels, shards(): pl.pallas_call(functools.partial(kernel, nz, ny), out_shape=(jax.ShapeDty...  117 us

profile of v3, /device:TPU:1, one launch (start us, length us, event | category | flops | bytes accessed | tf_op | source)
XLA Modules:
  0.0 120.7 jit_solution(10964051207719817749)
XLA Ops:
  0.6 116.6 %shard_map.50 = (f32[1,1]{1,0:T(1,128)}, f32[64,512]{1,0:T(8,128)}) custom-call(bf16[512,2048]{1,0:T(8,128)(2,1)} %x_hbm.1, bf16[64,512]{1,0:T(8,128)(2,1)} %w_hbm.1, bf16[512,512]{1,0:T(8,128)(2,1)} %t_hbm.1), custom_call_target="tpu_custom_call" | custom-call | tf_op jit(solution)/shard_map/pallas_call | solution.py:831
  118.0 1.6 %copy.8 = f32[64,512]{1,0:T(8,128)} copy(f32[64,512]{1,0:T(8,128)} %get-tuple-element.9) | data formatting | bytes 262144

commit v4 on v3

--- a/solution.py
+++ b/solution.py
@@ -21,11 +21,14 @@
 
 def kernel(
     nz, ny, x_hbm, w_hbm, t_hbm, loss_ref, g_ref,
-    x_ref, tb, tn, rl, xp, wb, pj, sT, cc, ca, cb, xs, xr, bs, br, sl, uu, gg, gs, gr, ga, gb, gxs, gxr, gcs, gcr,
+    x_ref, tb, tn, rl, xp, wb, pj, sT,
+    cc0, cc1, ca0, ca1, cb0, cb1, xs0, xs1, xr0, xr1, bs0, bs1, br0, br1, sl0, sl1, uu, gg, gs, gr, ga, gb, gxs, gxr, gcs, gcr,
     ar_t, ar_p, ar_u, ar_n, tst, nst, rowsum, lacc, lf, lc,
-    out_s, in_s, ar_s, ar_r, tc_r, tx_r, to_r, ty_r, xc_r, wc_r, wx_r, wz_r, wy_r,
-    ca_r, cx_r, cb_r, bx_r, sx_r, sz_r, sb_r, sy_r, ga_r, gx_r, gy_r, gb_r, gc_r, lc_r,
+    out_s, in_s, ar_s, ar_r, tc_r, tx_r, to_r, ty_r, xc_r, wc_r, wx_r, wz_r,
+    ca_r, cx_r, cb_r, bx_r, sx_r, sz_r, sr_r, sb_r, sy_r, ga_r, gx_r, gy_r, gb_r, gc_r, lc_r,
 ):
+    cc, ca, cb, xs = (cc0, cc1), (ca0, ca1), (cb0, cb1), (xs0, xs1)
+    xr, bs, br, sl = (xr0, xr1), (bs0, bs1), (br0, br1), (sl0, sl1)
     d = lax.axis_index("dp")
     f = lax.axis_index("feat")
     chips = 2 * nz
@@ -60,7 +63,7 @@
     x_prev = (cross, jnp.where(xl == 0, 1 - xh, xh) * ny + y)
 
     weigh = {}
-    CHIP, WEIGHT, TEACH, CROSS, CORR, GRAD = range(6)
+    CHIP, WEIGHT, TEACH, CROSS, CORR, GRAD, LAST = range(7)
 
     def copy(src, dst, s, r, to):
         return pltpu.make_async_remote_copy(
@@ -173,8 +176,8 @@
             for st in (dr,) if s == 0 else (0, 1):
                 v = local(st, p)
                 if s > 1 or (s == 1 and st == dr):
-                    v = v + buf[dr, s, st]
-                buf[dr, s, st] = v
+                    v = v + buf[dr, s, st].astype(F32)
+                buf[dr, s, st] = v.astype(buf.dtype)
             if s == 0:
                 send(kind, buf.at[dr, 0, dr], buf.at[dr, 1, dr], rs.at[dr, 0], hop(sgn))
             else:
@@ -185,7 +188,7 @@
             arrived(buf.at[dr, top], rs.at[dr, top - 1])
 
     def ring_total(st, buf, local):
-        return local(st, z) + buf[0, top, st] + buf[1, top, st]
+        return local(st, z) + buf[0, top, st].astype(F32) + buf[1, top, st].astype(F32)
 
     need = [top, 3, -3, 2, -2, 1, -1, 0]
 
@@ -275,19 +278,25 @@
     def t_hand(st, e):
         send(TEACH, t_at(st, e), tb.at[st, around(y + offs[e], ny), 1], tc_r.at[st, e], mate)
 
+    high, low = pl.ds(0, mid), pl.ds(mid, mid)
+
     def t_round(st, src):
-        send(TEACH, src, t_at(st, 0), ty_r.at[st, 0], right)
-        send(TEACH, src, t_at(st, 0), ty_r.at[st, 1], left)
+        there = t_at(st, 0)
+        send(TEACH, src.at[high], there.at[high], ty_r.at[st, 0], right)
+        send(TEACH, src.at[low], there.at[low], ty_r.at[st, 1], left)
+        send(TEACH, src.at[low], there.at[low], ty_r.at[st, 3], right)
+        send(TEACH, src.at[high], there.at[high], ty_r.at[st, 4], left)
 
     def t_pass(st):
-        arrived(t_at(st, 1), ty_r.at[st, 0])
-        high = t_at(st, 1).at[pl.ds(0, mid)]
-        send(TEACH, high, high, ty_r.at[st, 2], right)
-        arrived(t_at(st, 2), ty_r.at[st, 1])
-        low = t_at(st, 2).at[pl.ds(mid, mid)]
-        send(TEACH, low, low, ty_r.at[st, 2], left)
-        t_hand(st, 1)
-        t_hand(st, 2)
+        for e, part, to in ((1, high, right), (2, low, left)):
+            part = t_at(st, e).at[part]
+            arrived(part, ty_r.at[st, e - 1])
+            send(TEACH, part, part, ty_r.at[st, 2], to)
+
+    def t_near(st):
+        for e, part in ((1, low), (2, high)):
+            arrived(t_at(st, e).at[part], ty_r.at[st, e + 2])
+            t_hand(st, e)
 
     def t_far(st):
         arrived(t_at(st, 3), ty_r.at[st, 2])
@@ -312,7 +321,6 @@
         t_round(1, t_at(1, 0))
         t_hand(1, 0)
 
-    t_cross(0)
     t_round(0, t_hbm)
     send(CHIP, x_hbm, xp, xc_r, mate)
 
@@ -333,21 +341,16 @@
                 tn[st, p, pl.ds(there, 64), :] = ((v - center) * recip).astype(BF16)
 
     def w_own(p):
-        return wb.at[xl, p, 0]
+        return wb.at[xl, p]
 
     def w_other(p):
-        return wb.at[1 - xl, p, 0]
-
-    def w_late(p):
-        return wb.at[xl, p, 1]
-
-    w_like = wb.at[0, :, 0]
+        return wb.at[1 - xl, p]
 
     w_in.wait()
     arrived(wb.at[xl, z, 1 - core], wc_r)
     send(WEIGHT, w_own(z), w_own(z), wx_r, x_mate)
     ag_go(WEIGHT, w_own, wz_r.at[0])
-    agx_go(WEIGHT, w_late, wz_r.at[2], wy_r)
+    t_cross(0)
     t_cross(1)
 
     t_in.wait()
@@ -371,20 +374,20 @@
     ag_go(WEIGHT, w_other, wz_r.at[1])
     t_relay(0)
     ag_on(WEIGHT, w_own, wz_r.at[0], 0)
-    agx_on(WEIGHT, w_late, wz_r.at[2], wy_r, w_like)
+    t_pass(0)
     t_relay(1)
     ag_on(WEIGHT, w_other, wz_r.at[1], 1)
-    t_pass(0)
-    agx_end(WEIGHT, w_late, wz_r.at[2], wy_r, w_like)
     sums = ar_wait(ar_t, 0)
     center, recip = norm_of(sums[0:lanes], sums[lanes:2 * lanes])
     tst[f, 0:lanes, :] = center
     tst[f, lanes:2 * lanes, :] = recip
     f_start(tst, 3)
-    ag_end(w_like, wz_r.at[0])
-
+    t_near(0)
+
+    ag_end(wb.at[xl], wz_r.at[0])
     x_in.wait()
     arrived(xp, xc_r)
+    t_over()
     wide = wb.shape[1] * wb.shape[2] * wb.shape[3]
     tile = min(256, rows)
     tiles = rows // tile
@@ -409,9 +412,7 @@
 
     lax.fori_loop(0, tiles, project(x_ref, 0, xl, False), 0)
     lax.fori_loop(0, tiles, project(xp, rows, xl, False), 0)
-    t_over()
-    ag_end(w_like, wz_r.at[1])
-    arrived(wb.at[1 - xl, :, 1], wy_r)
+    ag_end(wb.at[1 - xl], wz_r.at[1])
     carry = lax.fori_loop(0, tiles, project(x_ref, 0, 1 - xl, True), (narrow, narrow))
     a, b = lax.fori_loop(0, tiles, project(xp, rows, 1 - xl, True), carry)
     ar_p[chip] = jnp.zeros((8, 128), F32)
@@ -433,6 +434,7 @@
     t_normal(0, 1)
     t_normal(0, 2)
 
+    t_normal(1, 0)
     sums = ar_wait(ar_p, 1)
     p_center, p_recip = norm_of(spread_out(sums, 0, half), spread_out(sums, lanes // 2, half))
     all_tiles = 2 * tiles
@@ -441,13 +443,20 @@
         pj[i * tile:(i + 1) * tile, :] = v
         sT[:, i * tile:(i + 1) * tile] = v.T.astype(BF16)
 
-    span = (ny // 2) * cols
+    def half_cols(h):
+        return pl.ds(pl.multiple_of(h * half, half), half)
 
     def correlate(g, h):
-        @pl.loop(0, ny // 2)
-        def _(j):
-            v = jnp.dot(sT[...], tn[g, h * (ny // 2) + j], preferred_element_type=F32)
-            cc[g, h, :, pl.ds(pl.multiple_of(j * cols, cols), cols)] = v
+        def block(ref, at, n):
+            cc[g][h, :, at:at + n] = jnp.dot(sT[...], ref, preferred_element_type=F32)
+
+        if g == 0:
+            for j in range(ny // 2):
+                block(tn[0, h * (ny // 2) + j], j * cols, cols)
+            block(tn[1, y, :, half_cols(h)], ny // 2 * cols, half)
+        else:
+            block(tn[1, around(y - 1 + 2 * h, ny)], 0, cols)
+            block(tn[1, around(y + 2, ny), :, half_cols(h)], cols, half)
 
     quarter = half // 2
     piece = quarter // nz
@@ -455,94 +464,142 @@
     def rows_of(a, p):
         return pl.ds(pl.multiple_of(a * quarter + p * piece, piece), piece)
 
-    side = span // 2
-
-    def sides(st):
+    def sides(g, st):
+        side = cc[g].shape[2] // 2
         return slice(st * side, (st + 1) * side)
 
     def ca_local(g):
-        return lambda st, p: cc[g, xl if st == 0 else 1 - xl, rows_of(0, p), :]
+        return lambda st, p: cc[g][xl if st == 0 else 1 - xl, rows_of(0, p), :]
 
     def ca_far(g):
-        far_step(CORR, ca.at[g], ca_local(g), ca_r.at[g])
+        far_step(CORR, ca[g], ca_local(g), ca_r.at[g, 0])
 
     def ca_mid(g):
-        mid_step(CORR, ca.at[g], ca_local(g), ca_r.at[g])
+        mid_step(CORR, ca[g], ca_local(g), ca_r.at[g, 0])
 
     def ca_near(g):
-        near_step(CORR, ca.at[g], ca_local(g), ca_r.at[g])
+        near_step(CORR, ca[g], ca_local(g), ca_r.at[g, 0])
+
+    def ca_ring(s):
+        ring_step(CORR, s, ca[0], ca_local(0), ca_r.at[0])
+
+    def ca_total(g, st):
+        return (ring_total, sum_total)[g](st, ca[g], ca_local(g))
 
     def ca_over(g):
-        sum_end(ca.at[g], ca_r.at[g])
-        xs[g] = sum_total(1, ca.at[g], ca_local(g)).astype(xs.dtype)
-        send(CORR, xs.at[g], xr.at[g], cx_r.at[g], x_mate)
+        (ring_end, sum_end)[g](ca[g], (ca_r.at[0], ca_r.at[1, 0])[g])
+        xs[g][...] = ca_total(g, 1).astype(BF16)
+        send(CORR, xs[g], xr[g], cx_r.at[g], x_mate)
 
     def cb_over(g):
-        bs[g] = cc[g, 1 - xl, quarter:half, :].astype(BF16).reshape(nz, piece, span)
+        bs[g][...] = cc[g][1 - xl, quarter:half, :].astype(BF16).reshape(bs[g].shape)
         for k in range(nz):
-            send(CORR, bs.at[g, need_at(k)], br.at[g, need_at(k)], bx_r.at[g, x_group(k)], x_mate)
+            send(CORR, bs[g].at[need_at(k)], br[g].at[need_at(k)], bx_r.at[g, (k + 1) // 2 if g == 0 else x_group(k)], x_mate)
 
     def cb_local(g):
-        return lambda st, p: cc[g, xl, rows_of(1, p), sides(st)] + br[g, p, :, sides(st)].astype(F32)
+        return lambda st, p: cc[g][xl, rows_of(1, p), sides(g, st)] + br[g][p, :, sides(g, st)].astype(F32)
+
+    def cb_ring(s):
+        arrived_all(br[0], 2 if 0 < s < top else 1, bx_r.at[0, s])
+        if s < top:
+            ring_step(CORR, s, cb[0], cb_local(0), cb_r.at[0])
+
+    def cb_total(g, st):
+        return (ring_total, sum_total)[g](st, cb[g], cb_local(g))
 
     def cb_far(g):
-        x_wait(0, br.at[g], bx_r.at[g])
-        far_step(CORR, cb.at[g], cb_local(g), cb_r.at[g])
+        x_wait(0, br[g], bx_r.at[g])
+        far_step(CORR, cb[g], cb_local(g), cb_r.at[g, 0])
 
     def cb_mid(g):
-        x_wait(1, br.at[g], bx_r.at[g])
-        mid_step(CORR, cb.at[g], cb_local(g), cb_r.at[g])
+        x_wait(1, br[g], bx_r.at[g])
+        mid_step(CORR, cb[g], cb_local(g), cb_r.at[g, 0])
 
     def cb_near(g):
-        x_wait(2, br.at[g], bx_r.at[g])
-        near_step(CORR, cb.at[g], cb_local(g), cb_r.at[g])
+        x_wait(2, br[g], bx_r.at[g])
+        near_step(CORR, cb[g], cb_local(g), cb_r.at[g, 0])
 
     def slope(a, g):
         if a == 0:
-            v = sum_total(0, ca.at[g], ca_local(g))
-            arrived(xr.at[g], cx_r.at[g])
-            v = v + xr[g].astype(F32)
+            v = ca_total(g, 0)
+            arrived(xr[g], cx_r.at[g])
+            v = v + xr[g][...].astype(F32)
         else:
-            sum_end(cb.at[g], cb_r.at[g])
-            x_wait(3, br.at[g], bx_r.at[g])
-            v = jnp.concatenate([sum_total(st, cb.at[g], cb_local(g)) for st in (0, 1)], axis=1)
+            (ring_end, sum_end)[g](cb[g], (cb_r.at[0], cb_r.at[1, 0])[g])
+            if g == 0:
+                cb_ring(top)
+            else:
+                x_wait(3, br[g], bx_r.at[g])
+            v = jnp.concatenate([cb_total(g, st) for st in (0, 1)], axis=1)
         share = v / total_rows
         student_index = (
             f * cols + core * half + a * quarter + z * piece
             + lax.broadcasted_iota(jnp.int32, share.shape, 0)
         )
-        group = xh if g == 0 else 1 - xh
-        teacher_index = (group * 2 + xl) * span + lax.broadcasted_iota(jnp.int32, share.shape, 1)
+        col = lax.broadcasted_iota(jnp.int32, share.shape, 1)
+        whole = ny // 2 * cols
+        teacher_index = jnp.where(col < whole, (xh * 2 + xl) * whole + col, -1) if g == 0 else -1 - col
         on_diag = student_index == teacher_index
         part = jnp.where(on_diag, (1.0 - share) ** 2, OFF_WEIGHT * share * share)
-        lacc[g, a] = jnp.sum(part.reshape(piece // 8, 8, span), axis=0)
+        part = jnp.sum(part.reshape(piece // 8, 8, part.shape[1]), axis=0)
+        lacc[g, a] = sum(part[:, k:k + 128] for k in range(0, part.shape[1], 128))
         lean = jnp.where(on_diag, -2.0 * (1.0 - share), 2.0 * OFF_WEIGHT * share).astype(BF16)
-        sl[g, xl, a, z] = lean
+        sl[g][xl, a, z] = lean
         lean = lean.astype(F32)
-        at = group * ny + xl * (ny // 2)
-        n_row = jnp.concatenate([spread_out(nst[at + k], 0, cols) for k in range(ny // 2)], axis=1)
+        other = (1 - xh) * ny
+        if g == 0:
+            at = xh * ny + xl * (ny // 2)
+            blocks, last = [at + k for k in range(ny // 2)], other + y
+        else:
+            blocks, last = [other + around(y - 1 + 2 * xl, ny)], other + around(y + 2, ny)
+        n_row = [spread_out(nst[b], 0, cols) for b in blocks]
+        last = spread_out(nst[last], 0, cols)
+        n_row.append(jnp.where(xl == 0, last[:, 0:half], last[:, half:cols]))
+        n_row = jnp.concatenate(n_row, axis=1)
         here = pl.ds(pl.multiple_of(z * piece, piece), piece)
         for k, v in ((a, lean * n_row), (2 + a, lean * share)):
             v = jnp.broadcast_to(jnp.sum(v, axis=1, keepdims=True), (piece, 128))
             rowsum[k, here, :] = v if g == 0 else rowsum[k, here, :] + v
+
+    def slope_go(a, g):
         if (a, g) == (0, 1):
-            there = sl.at[g, xl, 0, z]
+            there = sl[g].at[xl, 0, z]
             send(CORR, there, there, sx_r, x_mate)
             ag_go(CORR, sa_own(g), sz_r.at[0])
         else:
-            agx_go(CORR, sb_own(a, g), sb_r.at[g, a], sy_r.at[g, a])
+            if g == 0:
+                s_ring(a, 0)
+            else:
+                agx_go(CORR, sb_own(a, g), sb_r, sy_r.at[g, a])
+
+    def s_ring(a, s):
+        own = sb_own(a, 0)
+        side = sl[0].shape[-1] // 2
+        if s == 0:
+            agx_to(CORR, own, sy_r.at[0, a], (0,))
+        for dr in (0, 1):
+            sgn = 1 - 2 * dr
+            block = own(around(z - sgn * s, nz))
+            half_of = block.at[:, pl.ds(dr * side, side)]
+            if s > 0:
+                arrived(block if s < top else half_of, sr_r.at[a, dr, s - 1])
+            if s < top:
+                part = block if s < top - 1 else half_of
+                send(CORR, part, part, sr_r.at[a, dr, s], hop(sgn))
+        if s > 0:
+            agx_to(CORR, own, sy_r.at[0, a], (-s, s) if s < top else (top,))
 
     def sa_own(g):
-        return lambda p: sl.at[g, xl, 0, p]
+        return lambda p: sl[g].at[xl, 0, p]
 
     def sa_mate(g):
-        return lambda p: sl.at[g, 1 - xl, 0, p]
+        return lambda p: sl[g].at[1 - xl, 0, p]
 
     def sb_own(a, g):
-        return lambda p: sl.at[g, xl, a, p]
+        return lambda p: sl[g].at[xl, a, p]
 
     def sa_other(g):
-        arrived(sl.at[g, 1 - xl, 0, z], sx_r)
+        arrived(sl[g].at[1 - xl, 0, z], sx_r)
         ag_go(CORR, sa_mate(g), sz_r.at[1])
 
     def sa_on(g):
@@ -552,42 +609,48 @@
         ag_on(CORR, sa_mate(g), sz_r.at[1], 1)
 
     def sa_end(g):
-        ag_end(sl.at[g, 0, 0], sz_r.at[0])
-        ag_end(sl.at[g, 0, 0], sz_r.at[1])
+        ag_end(sl[g].at[0, 0], sz_r.at[0])
+        ag_end(sl[g].at[0, 0], sz_r.at[1])
 
     def sb_on(a, g):
-        agx_on(CORR, sb_own(a, g), sb_r.at[g, a], sy_r.at[g, a], sl.at[g, xl, a])
+        agx_on(CORR, sb_own(a, g), sb_r, sy_r.at[g, a], sl[g].at[xl, a])
 
     def sb_end(a, g):
-        agx_end(CORR, sb_own(a, g), sb_r.at[g, a], sy_r.at[g, a], sl.at[g, xl, a])
+        agx_end(CORR, sb_own(a, g), sb_r, sy_r.at[g, a], sl[g].at[xl, a])
 
     def sb_last(a, g):
-        arrived(sl.at[g, 1 - xl, a], sy_r.at[g, a])
+        arrived(sl[g].at[1 - xl, a], sy_r.at[g, a])
 
     def row_tile(i):
         return pl.ds(pl.multiple_of(i * tile, tile), tile)
 
-    def times_slope(v, g, here):
-        for j in range(ny):
-            h, k = j // (ny // 2), j % (ny // 2)
-            rhs = sl[g, h, :, :, :, k * cols:(k + 1) * cols].reshape(half, cols)
-            w = lax.dot_general(
-                tn[g, j, here, :], rhs, (((1,), (1,)), ((), ())), preferred_element_type=F32
-            )
+    def times_slope(v, g, h, here):
+        if g == 0:
+            terms = [(tn[0, h * (ny // 2) + j, here, :], j * cols, cols) for j in range(ny // 2)]
+            terms.append((tn[1, y, here, half_cols(h)], ny // 2 * cols, half))
+        else:
+            terms = [(tn[1, around(y - 1 + 2 * h, ny), here, :], 0, cols)]
+            terms.append((tn[1, around(y + 2, ny), here, half_cols(h)], cols, half))
+        for lhs, at, n in terms:
+            rhs = sl[g][h, :, :, :, at:at + n].reshape(half, n)
+            w = lax.dot_general(lhs, rhs, (((1,), (1,)), ((), ())), preferred_element_type=F32)
             v = w if v is None else v + w
         return v
 
-    def upstream_first():
+    def upstream(first, *parts):
         @pl.loop(0, all_tiles)
         def _(i):
-            uu[row_tile(i), :] = times_slope(None, 0, row_tile(i))
+            v = None if first else uu[row_tile(i), :]
+            for g, h in parts:
+                v = times_slope(v, g, h, row_tile(i))
+            uu[row_tile(i), :] = v
 
     def u_start():
         for k in range(4):
             ar_u[chip, k:k + 1, :] = rowsum[k].T[0:1]
-        part = jnp.sum(lacc[0, 0] + lacc[0, 1] + lacc[1, 0] + lacc[1, 1], axis=0, keepdims=True)
-        part = sum(part[:, k * cols:(k + 1) * cols] for k in range(span // cols))
-        pack(ar_u, chip, lanes, part)
+        ar_u[chip, lanes:2 * lanes, :] = jnp.zeros((lanes, 128), F32)
+        part = lacc[0, 0] + lacc[0, 1] + lacc[1, 0] + lacc[1, 1]
+        ar_u[chip, lanes:lanes + 1, :] = jnp.sum(part, axis=0, keepdims=True)
         ar_start(ar_u, 2)
 
     def delta():
@@ -598,14 +661,13 @@
         @pl.loop(0, all_tiles)
         def _(i):
             here = row_tile(i)
-            v = times_slope(uu[here, :], 1, here) / total_rows
+            v = times_slope(uu[here, :], 1, 1 - xl, here) / total_rows
             v = p_recip * (v - mean_g - pj[here, :] * mean_x)
             sT[:, pl.ds(pl.multiple_of(i * tile, tile), tile)] = v.T.astype(BF16)
 
         return sums
 
-    strip = gg.shape[3]
-    band = quarter // 2
+    strip = gg.shape[2]
 
     def gradient(h, out):
         @pl.loop(0, nz // 2)
@@ -613,14 +675,15 @@
             here = pl.ds(pl.multiple_of(h * nz * strip + j * 2 * strip, 2 * strip), 2 * strip)
             v = jnp.dot(sT[:, 0:rows], x_ref[:, here], preferred_element_type=F32)
             v = v + jnp.dot(sT[:, rows:2 * rows], xp[:, here], preferred_element_type=F32)
-            v = v.astype(out.dtype)
-            for a in (0, 1):
-                for k in (0, 1):
-                    out[a, 2 * j + k] = v[a * quarter:(a + 1) * quarter, k * strip:(k + 1) * strip]
+            for k in (0, 1):
+                out[2 * j + k] = v[:, k * strip:(k + 1) * strip]
+
+    band, wide_band = ga.shape[4], gb.shape[3]
+    split = 2 * band
 
     def ga_local(i):
         part = slice(i * band, (i + 1) * band)
-        return lambda st, p: (gg if st == 0 else gs)[0, p, part, :]
+        return lambda st, p: (gg if st == 0 else gs)[p, part, :]
 
     def ga_step(s):
         for i in (0, 1):
@@ -634,97 +697,101 @@
 
     def gb_over():
         for k in range(nz):
-            send(GRAD, gs.at[1, need_at(k)], gr.at[need_at(k)], gy_r.at[x_group(k)], x_mate)
+            part = gs.at[need_at(k), pl.ds(split, half - split)]
+            send(GRAD, part, gr.at[need_at(k)], gy_r.at[(k + 1) // 2], x_mate)
+
+    def gb_wait(s):
+        arrived_all(gr, 2 if 0 < s < top else 1, gy_r.at[s])
 
     def gb_local(st, p):
-        part = slice(st * band, (st + 1) * band)
-        return gg[1, p, part, :] + gr[p, part, :]
-
-    def gb_far():
-        x_wait(0, gr, gy_r)
-        far_step(GRAD, gb, gb_local, gb_r)
-
-    def gb_mid():
-        x_wait(1, gr, gy_r)
-        mid_step(GRAD, gb, gb_local, gb_r)
-
-    def gb_near():
-        x_wait(2, gr, gy_r)
-        near_step(GRAD, gb, gb_local, gb_r)
+        low = st * wide_band
+        return gg[p, split + low:split + low + wide_band, :] + gr[p, low:low + wide_band, :]
+
+    def gb_step(s):
+        gb_wait(s)
+        ring_step(GRAD, s, gb, gb_local, gb_r)
 
     mine = strip // 2
     first = core == 0
 
-    def g_core(a):
-        if a == 0:
-            parts = []
-            for i in (0, 1):
-                v = ring_total(0, ga.at[i], ga_local(i))
-                arrived(gxr.at[i], gx_r.at[i])
-                parts.append(v + gxr[i])
-        else:
-            sum_end(gb, gb_r)
-            x_wait(3, gr, gy_r)
-            parts = [sum_total(st, gb, gb_local) for st in (0, 1)]
-        v = jnp.concatenate(parts, axis=0)
-        v = (LOSS_SCALE * v).T
+    def g_core():
+        parts = []
+        for i in (0, 1):
+            v = ring_total(0, ga.at[i], ga_local(i))
+            arrived(gxr.at[i], gx_r.at[i])
+            parts.append(v + gxr[i])
+        ring_end(gb, gb_r)
+        gb_wait(top)
+        parts += [ring_total(st, gb, gb_local) for st in (0, 1)]
+        v = (LOSS_SCALE * jnp.concatenate(parts, axis=0)).T
         low, high = v[0:mine], v[mine:strip]
-        gcs[a] = jnp.where(first, high, low)
-        send(GRAD, gcs.at[a], gcr.at[a], gc_r.at[a], mate)
-        g_ref[:, pl.ds(pl.multiple_of(core * half + a * quarter, quarter), quarter)] = jnp.where(first, low, high)
-
-    def g_last(a):
-        arrived(gcr.at[a], gc_r.at[a])
-        g_ref[:, pl.ds(pl.multiple_of((1 - core) * half + a * quarter, quarter), quarter)] = gcr[a]
+        gcs[...] = jnp.where(first, high, low)
+        send(LAST, gcs, gcr, gc_r, mate)
+        g_ref[:, my_cols] = jnp.where(first, low, high)
+
+    def g_last():
+        arrived(gcr, gc_r)
+        g_ref[:, mate_cols] = gcr[...]
 
     t_normal(0, 3)
+    t_pass(1)
     correlate(0, 1 - xl)
     cb_over(0)
     correlate(0, xl)
-    ca_far(0)
-    ca_near(0)
-    t_normal(1, 0)
+    ca_ring(0)
     nst[f] = ar_wait(ar_n, 5)
     f_start(nst, 6)
-    cb_far(0)
-    ca_mid(0)
-    t_pass(1)
-    cb_mid(0)
-    cb_near(0)
-    ca_over(0)
+    cb_ring(0)
+    ca_ring(1)
+    t_near(1)
+    cb_ring(1)
+    ca_ring(2)
+    cb_ring(2)
+    t_far(1)
     t_normal(1, 1)
     t_normal(1, 2)
-    t_far(1)
-    f_wait(nst, 6)
-    slope(1, 0)
-    slope(0, 0)
+    ca_ring(3)
     t_normal(1, 3)
+    cb_ring(3)
     correlate(1, 1 - xl)
     cb_over(1)
     correlate(1, xl)
     ca_far(1)
     ca_near(1)
+    ca_over(0)
     cb_far(1)
     ca_mid(1)
-    sb_on(0, 0)
-    sb_on(1, 0)
+    f_wait(nst, 6)
+    slope(1, 0)
+    slope(0, 0)
+    slope_go(0, 0)
     cb_mid(1)
+    slope_go(1, 0)
     cb_near(1)
     ca_over(1)
-    sb_end(0, 0)
-    sb_end(1, 0)
+    s_ring(0, 1)
+    s_ring(1, 1)
     slope(0, 1)
+    slope_go(0, 1)
+    s_ring(0, 2)
     slope(1, 1)
+    slope_go(1, 1)
     u_start()
+    s_ring(1, 2)
     sa_other(1)
+    s_ring(0, 3)
     sa_on(1)
+    s_ring(1, 3)
     sb_on(1, 1)
+    s_ring(0, 4)
     sa_on_other(1)
+    s_ring(1, 4)
+    sb_end(1, 1)
+    upstream(True, (0, xl))
+    sa_end(1)
     sb_last(0, 0)
     sb_last(1, 0)
-    upstream_first()
-    sb_end(1, 1)
-    sa_end(1)
+    upstream(False, (1, xl), (0, 1 - xl))
     sb_last(1, 1)
     sums = delta()
     gradient(1 - xl, gs)
@@ -733,22 +800,21 @@
     ga_step(0)
     lf[f] = jnp.broadcast_to(jnp.sum(sums[lanes:2 * lanes], axis=0, keepdims=True), (8, 128))
     f_start(lf, 4)
+    gb_step(0)
     ga_step(1)
-    gb_far()
+    gb_step(1)
     ga_step(2)
-    gb_mid()
+    gb_step(2)
     ga_step(3)
-    gb_near()
+    gb_step(3)
     f_wait(lf, 4)
     lc[0] = jnp.sum(lf[...], axis=0)
     copy(lc.at[0], lc.at[1], ar_s.at[7], lc_r, mate).start()
     ga_over()
-    g_core(1)
-    g_core(0)
+    g_core()
     arrived(lc.at[1], lc_r)
     loss_ref[0, 0] = jnp.sum((lc[0] + lc[1])[0:1]) / width_all
-    g_last(1)
-    g_last(0)
+    g_last()
     ar_sent(ar_t, 0, chips)
     ar_sent(ar_p, 1, chips)
     ar_sent(ar_u, 2, chips)
@@ -758,11 +824,11 @@
     ar_sent(lf, 4, feats)
     copy(lc.at[0], lc.at[1], ar_s.at[7], lc_r, mate).wait_send()
     for kind, size in weigh.items():
-        there = {WEIGHT: pj, TEACH: tn, CORR: cc}.get(kind, cc.at[0])
+        there = pj if kind in (WEIGHT, LAST) else tn
         line = there.dtype.itemsize
         for n in there.shape[:-2] + there.shape[-1:]:
             line *= n
-        assert size % line == 0 and size // line % 8 == 0
+        assert size % line == 0 and size // line % 16 == 0
         there = there.at[(slice(None),) * (len(there.shape) - 2) + (pl.ds(0, size // line),)]
         copy(there, there, out_s.at[kind], lc_r, mate).wait_send()
 
@@ -771,11 +837,12 @@
     rows, wide = student.shape
     strip_w, cols = weight.shape
     half = cols // 2
-    span = (ny // 2) * cols
+    spans = ((ny + 1) * cols // 2, (ny - 1) * cols // 2)
     chips, feats = 2 * nz, 2 * ny
     strip = wide // chips
     quarter = half // 2
     piece = quarter // nz
+    band = 7 * half // 32
     V = pltpu.VMEM
     D = pltpu.SemaphoreType.DMA
     data = [
@@ -787,24 +854,26 @@
         V((2, nz, 2, strip_w, half), BF16),
         V((2 * rows, half), F32),
         V((half, 2 * rows), BF16),
-        V((2, 2, half, span), F32),
-        V((2, 2, 7, 3, piece, span), BF16),
-        V((2, 2, 7, 3, piece, span // 2), BF16),
-        V((2, piece, span), BF16),
-        V((2, piece, span), BF16),
-        V((2, nz, piece, span), BF16),
-        V((2, nz, piece, span), BF16),
-        V((2, 2, 2, nz, piece, span), BF16),
+        *[V((2, half, n), F32) for n in spans],
+        V((2, nz // 2 + 1, 2, piece, spans[0]), BF16),
+        V((2, 7, 3, piece, spans[1]), BF16),
+        V((2, nz // 2 + 1, 2, piece, spans[0] // 2), BF16),
+        V((2, 7, 3, piece, spans[1] // 2), BF16),
+        *[V((piece, n), BF16) for n in spans],
+        *[V((piece, n), BF16) for n in spans],
+        *[V((nz, piece, n), BF16) for n in spans],
+        *[V((nz, piece, n), BF16) for n in spans],
+        *[V((2, 2, nz, piece, n), BF16) for n in spans],
         V((2 * rows, half), F32),
-        V((2, nz, quarter, strip), F32),
-        V((2, nz, quarter, strip), F32),
-        V((nz, quarter, strip), F32),
-        V((2, 2, nz // 2 + 1, 2, quarter // 2, strip), F32),
-        V((2, 7, 3, quarter // 2, strip), F32),
-        V((2, quarter // 2, strip), F32),
-        V((2, quarter // 2, strip), F32),
-        V((2, strip // 2, quarter), F32),
-        V((2, strip // 2, quarter), F32),
+        V((nz, half, strip), F32),
+        V((nz, half, strip), F32),
+        V((nz, half - 2 * band, strip), F32),
+        V((2, 2, nz // 2 + 1, 2, band, strip), F32),
+        V((2, nz // 2 + 1, 2, half // 2 - band, strip), F32),
+        V((2, band, strip), F32),
+        V((2, band, strip), F32),
+        V((strip // 2, half), F32),
+        V((strip // 2, half), F32),
         V((chips, 8, 128), F32),
         V((chips, 8, 128), F32),
         V((chips, 8, 128), F32),
@@ -812,17 +881,17 @@
         V((feats, 8, 128), F32),
         V((feats, 8, 128), F32),
         V((4, 128, 128), F32),
-        V((2, 2, 8, span), F32),
+        V((2, 2, 8, 128), F32),
         V((feats, 8, 128), F32),
         V((2, 8, 128), F32),
     ]
     sems = [
         D(shape) for shape in (
-            (6,), (3,), (8,), (7,),
-            (2, ny), (2, 2), (), (2, 3), (), (), (), (3, 4), (),
-            (2, 3), (2,), (2, 3), (2, 4),
-            (), (2, 4), (2, 2, 4), (2, 2),
-            (2, 2, nz // 2), (2,), (4,), (3,), (2,), (),
+            (7,), (3,), (8,), (7,),
+            (2, ny), (2, 2), (), (2, 5), (), (), (), (2, 4),
+            (2, 2, nz // 2), (2,), (2, 2, nz // 2), (2, 5),
+            (), (2, 4), (2, 2, nz // 2), (4,), (2, 2),
+            (2, 2, nz // 2), (2,), (5,), (2, nz // 2), (), (),
         )
     ]
     vm = pl.BlockSpec(memory_space=pltpu.VMEM)

time: 121 us -> 114 us (0.942)
  Pallas kernels: 117 us -> 110 us
    pallas_call x1, Pallas kernels: 117 us -> 110 us  [shards(): pl.pallas_call(functools.partial(kernel, nz, ny), out_shape=(jax.ShapeDty...]
where the time goes in v4:
time: 114 us
  Pallas kernels  110 us (96%)
  between operations  2.45 us (2%)
  local copies, waits for them, and re-layouts  1.57 us (1%)
    pallas_call x1, Pallas kernels, shards(): pl.pallas_call(functools.partial(kernel, nz, ny), out_shape=(jax.ShapeDty...  110 us

profile of v4, /device:TPU:1, one launch (start us, length us, event | category | flops | bytes accessed | tf_op | source)
XLA Modules:
  0.0 114.1 jit_solution(15673761187440587398)
XLA Ops:
  0.6 110.1 %shard_map.50 = (f32[1,1]{1,0:T(1,128)}, f32[64,512]{1,0:T(8,128)}) custom-call(bf16[512,2048]{1,0:T(8,128)(2,1)} %x_hbm.1, bf16[64,512]{1,0:T(8,128)(2,1)} %w_hbm.1, bf16[512,512]{1,0:T(8,128)(2,1)} %t_hbm.1), custom_call_target="tpu_custom_call" | custom-call | tf_op jit(solution)/shard_map/pallas_call | solution.py:900
  111.4 1.6 %copy.8 = f32[64,512]{1,0:T(8,128)} copy(f32[64,512]{1,0:T(8,128)} %get-tuple-element.9) | data formatting | bytes 262144

commit v5 on v4

--- a/solution.py
+++ b/solution.py
@@ -435,6 +435,7 @@
     t_normal(0, 2)
 
     t_normal(1, 0)
+    t_normal(0, 3)
     sums = ar_wait(ar_p, 1)
     p_center, p_recip = norm_of(spread_out(sums, 0, half), spread_out(sums, lanes // 2, half))
     all_tiles = 2 * tiles
@@ -637,10 +638,10 @@
             v = w if v is None else v + w
         return v
 
-    def upstream(first, *parts):
+    def upstream(*parts):
         @pl.loop(0, all_tiles)
         def _(i):
-            v = None if first else uu[row_tile(i), :]
+            v = None
             for g, h in parts:
                 v = times_slope(v, g, h, row_tile(i))
             uu[row_tile(i), :] = v
@@ -661,7 +662,8 @@
         @pl.loop(0, all_tiles)
         def _(i):
             here = row_tile(i)
-            v = times_slope(uu[here, :], 1, 1 - xl, here) / total_rows
+            v = times_slope(uu[here, :], 0, 1 - xl, here)
+            v = times_slope(v, 1, 1 - xl, here) / total_rows
             v = p_recip * (v - mean_g - pj[here, :] * mean_x)
             sT[:, pl.ds(pl.multiple_of(i * tile, tile), tile)] = v.T.astype(BF16)
 
@@ -669,9 +671,10 @@
 
     strip = gg.shape[2]
 
-    def gradient(h, out):
-        @pl.loop(0, nz // 2)
+    def gradient(h, out, *pairs):
+        @pl.loop(*pairs)
         def _(j):
+            j = lax.rem(lax.div(z, 2) + top // 2 + j, nz // 2)
             here = pl.ds(pl.multiple_of(h * nz * strip + j * 2 * strip, 2 * strip), 2 * strip)
             v = jnp.dot(sT[:, 0:rows], x_ref[:, here], preferred_element_type=F32)
             v = v + jnp.dot(sT[:, rows:2 * rows], xp[:, here], preferred_element_type=F32)
@@ -695,8 +698,8 @@
             gxs[i] = ring_total(1, ga.at[i], ga_local(i))
             send(GRAD, gxs.at[i], gxr.at[i], gx_r.at[i], x_mate)
 
-    def gb_over():
-        for k in range(nz):
+    def gb_over(*ks):
+        for k in ks:
             part = gs.at[need_at(k), pl.ds(split, half - split)]
             send(GRAD, part, gr.at[need_at(k)], gy_r.at[(k + 1) // 2], x_mate)
 
@@ -733,7 +736,6 @@
         arrived(gcr, gc_r)
         g_ref[:, mate_cols] = gcr[...]
 
-    t_normal(0, 3)
     t_pass(1)
     correlate(0, 1 - xl)
     cb_over(0)
@@ -746,17 +748,17 @@
     t_near(1)
     cb_ring(1)
     ca_ring(2)
+    t_far(1)
     cb_ring(2)
-    t_far(1)
     t_normal(1, 1)
     t_normal(1, 2)
     ca_ring(3)
     t_normal(1, 3)
-    cb_ring(3)
     correlate(1, 1 - xl)
     cb_over(1)
     correlate(1, xl)
     ca_far(1)
+    cb_ring(3)
     ca_near(1)
     ca_over(0)
     cb_far(1)
@@ -779,25 +781,27 @@
     u_start()
     s_ring(1, 2)
     sa_other(1)
+    sa_on(1)
     s_ring(0, 3)
-    sa_on(1)
+    sb_on(1, 1)
     s_ring(1, 3)
-    sb_on(1, 1)
+    sa_on_other(1)
     s_ring(0, 4)
-    sa_on_other(1)
     s_ring(1, 4)
     sb_end(1, 1)
-    upstream(True, (0, xl))
     sa_end(1)
+    upstream((0, xl), (1, xl))
     sb_last(0, 0)
     sb_last(1, 0)
-    upstream(False, (1, xl), (0, 1 - xl))
     sb_last(1, 1)
     sums = delta()
-    gradient(1 - xl, gs)
-    gb_over()
-    gradient(xl, gg)
+    gradient(1 - xl, gs, 0, 1)
+    gb_over(0)
+    gradient(xl, gg, 0, 1)
     ga_step(0)
+    gradient(1 - xl, gs, 1, nz // 2)
+    gb_over(1, 2, 3, 4, 5, 6, 7)
+    gradient(xl, gg, 1, nz // 2)
     lf[f] = jnp.broadcast_to(jnp.sum(sums[lanes:2 * lanes], axis=0, keepdims=True), (8, 128))
     f_start(lf, 4)
     gb_step(0)

time: 114 us -> 113 us (level)
    pallas_call x1, Pallas kernels: 110 us -> 109 us  [shards(): pl.pallas_call(functools.partial(kernel, nz, ny), out_shape=(jax.ShapeDty...]
where the time goes in v5:
time: 113 us
  Pallas kernels  109 us (96%)
  between operations  2.45 us (2%)
  local copies, waits for them, and re-layouts  1.57 us (1%)
    pallas_call x1, Pallas kernels, shards(): pl.pallas_call(functools.partial(kernel, nz, ny), out_shape=(jax.ShapeDty...  109 us

profile of v5, /device:TPU:1, one launch (start us, length us, event | category | flops | bytes accessed | tf_op | source)
XLA Modules:
  0.0 113.0 jit_solution(466442637641730731)
XLA Ops:
  0.6 108.9 %shard_map.50 = (f32[1,1]{1,0:T(1,128)}, f32[64,512]{1,0:T(8,128)}) custom-call(bf16[512,2048]{1,0:T(8,128)(2,1)} %x_hbm.1, bf16[64,512]{1,0:T(8,128)(2,1)} %w_hbm.1, bf16[512,512]{1,0:T(8,128)(2,1)} %t_hbm.1), custom_call_target="tpu_custom_call" | custom-call | tf_op jit(solution)/shard_map/pallas_call | solution.py:904
  110.3 1.6 %copy.8 = f32[64,512]{1,0:T(8,128)} copy(f32[64,512]{1,0:T(8,128)} %get-tuple-element.9) | data formatting | bytes 262144

commit v6 on v5

--- a/solution.py
+++ b/solution.py
@@ -166,26 +166,25 @@
         return v
 
     def ring_step(kind, s, buf, local, rs):
+        if s == 1:
+            arrived(buf.at[0, s], rs.at[s - 1])
+        elif s > 1:
+            arrived(buf.at[:, s], rs.at[s - 1])
         for dr in (0, 1):
             sgn = 1 - 2 * dr
             p = around(z + sgn * (top - s), nz)
-            if s == 1:
-                arrived(buf.at[dr, s, dr], rs.at[dr, s - 1])
-            elif s > 1:
-                arrived(buf.at[dr, s], rs.at[dr, s - 1])
             for st in (dr,) if s == 0 else (0, 1):
                 v = local(st, p)
                 if s > 1 or (s == 1 and st == dr):
                     v = v + buf[dr, s, st].astype(F32)
                 buf[dr, s, st] = v.astype(buf.dtype)
             if s == 0:
-                send(kind, buf.at[dr, 0, dr], buf.at[dr, 1, dr], rs.at[dr, 0], hop(sgn))
+                send(kind, buf.at[dr, 0, dr], buf.at[dr, 1, dr], rs.at[0], hop(sgn))
             else:
-                send(kind, buf.at[dr, s], buf.at[dr, s + 1], rs.at[dr, s], hop(sgn))
+                send(kind, buf.at[dr, s], buf.at[dr, s + 1], rs.at[s], hop(sgn))
 
     def ring_end(buf, rs):
-        for dr in (0, 1):
-            arrived(buf.at[dr, top], rs.at[dr, top - 1])
+        arrived(buf.at[:, top], rs.at[top - 1])
 
     def ring_total(st, buf, local):
         return local(st, z) + buf[0, top, st].astype(F32) + buf[1, top, st].astype(F32)
@@ -204,8 +203,10 @@
     def ar_copy(buf, i, k):
         return copy(buf.at[chip], buf.at[chip], ar_s.at[i], ar_r.at[i], dp_at(around(chip + k, chips)))
 
+    farthest = sorted(range(1, chips), key=lambda k: -min(k % nz, nz - k % nz))
+
     def ar_start(buf, i):
-        for k in range(1, chips):
+        for k in farthest:
             ar_copy(buf, i, k).start()
 
     def ar_wait(buf, i):
@@ -473,13 +474,13 @@
         return lambda st, p: cc[g][xl if st == 0 else 1 - xl, rows_of(0, p), :]
 
     def ca_far(g):
-        far_step(CORR, ca[g], ca_local(g), ca_r.at[g, 0])
+        far_step(CORR, ca[g], ca_local(g), ca_r.at[g])
 
     def ca_mid(g):
-        mid_step(CORR, ca[g], ca_local(g), ca_r.at[g, 0])
+        mid_step(CORR, ca[g], ca_local(g), ca_r.at[g])
 
     def ca_near(g):
-        near_step(CORR, ca[g], ca_local(g), ca_r.at[g, 0])
+        near_step(CORR, ca[g], ca_local(g), ca_r.at[g])
 
     def ca_ring(s):
         ring_step(CORR, s, ca[0], ca_local(0), ca_r.at[0])
@@ -488,7 +489,7 @@
         return (ring_total, sum_total)[g](st, ca[g], ca_local(g))
 
     def ca_over(g):
-        (ring_end, sum_end)[g](ca[g], (ca_r.at[0], ca_r.at[1, 0])[g])
+        (ring_end, sum_end)[g](ca[g], ca_r.at[g])
         xs[g][...] = ca_total(g, 1).astype(BF16)
         send(CORR, xs[g], xr[g], cx_r.at[g], x_mate)
 
@@ -510,15 +511,15 @@
 
     def cb_far(g):
         x_wait(0, br[g], bx_r.at[g])
-        far_step(CORR, cb[g], cb_local(g), cb_r.at[g, 0])
+        far_step(CORR, cb[g], cb_local(g), cb_r.at[g])
 
     def cb_mid(g):
         x_wait(1, br[g], bx_r.at[g])
-        mid_step(CORR, cb[g], cb_local(g), cb_r.at[g, 0])
+        mid_step(CORR, cb[g], cb_local(g), cb_r.at[g])
 
     def cb_near(g):
         x_wait(2, br[g], bx_r.at[g])
-        near_step(CORR, cb[g], cb_local(g), cb_r.at[g, 0])
+        near_step(CORR, cb[g], cb_local(g), cb_r.at[g])
 
     def slope(a, g):
         if a == 0:
@@ -526,7 +527,7 @@
             arrived(xr[g], cx_r.at[g])
             v = v + xr[g][...].astype(F32)
         else:
-            (ring_end, sum_end)[g](cb[g], (cb_r.at[0], cb_r.at[1, 0])[g])
+            (ring_end, sum_end)[g](cb[g], cb_r.at[g])
             if g == 0:
                 cb_ring(top)
             else:
@@ -717,24 +718,26 @@
     mine = strip // 2
     first = core == 0
 
-    def g_core():
+    def g_core(a):
         parts = []
-        for i in (0, 1):
-            v = ring_total(0, ga.at[i], ga_local(i))
-            arrived(gxr.at[i], gx_r.at[i])
-            parts.append(v + gxr[i])
-        ring_end(gb, gb_r)
-        gb_wait(top)
-        parts += [ring_total(st, gb, gb_local) for st in (0, 1)]
+        if a == 0:
+            for i in (0, 1):
+                v = ring_total(0, ga.at[i], ga_local(i))
+                arrived(gxr.at[i], gx_r.at[i])
+                parts.append(v + gxr[i])
+        else:
+            ring_end(gb, gb_r)
+            gb_wait(top)
+            parts = [ring_total(st, gb, gb_local) for st in (0, 1)]
         v = (LOSS_SCALE * jnp.concatenate(parts, axis=0)).T
         low, high = v[0:mine], v[mine:strip]
-        gcs[...] = jnp.where(first, high, low)
-        send(LAST, gcs, gcr, gc_r, mate)
-        g_ref[:, my_cols] = jnp.where(first, low, high)
-
-    def g_last():
-        arrived(gcr, gc_r)
-        g_ref[:, mate_cols] = gcr[...]
+        gcs[a] = jnp.where(first, high, low)
+        send(LAST, gcs.at[a], gcr.at[a], gc_r.at[a], mate)
+        g_ref[:, pl.ds(pl.multiple_of(core * half + a * quarter, quarter), quarter)] = jnp.where(first, low, high)
+
+    def g_last(a):
+        arrived(gcr.at[a], gc_r.at[a])
+        g_ref[:, pl.ds(pl.multiple_of((1 - core) * half + a * quarter, quarter), quarter)] = gcr[a]
 
     t_pass(1)
     correlate(0, 1 - xl)
@@ -815,10 +818,12 @@
     lc[0] = jnp.sum(lf[...], axis=0)
     copy(lc.at[0], lc.at[1], ar_s.at[7], lc_r, mate).start()
     ga_over()
-    g_core()
+    g_core(1)
+    g_core(0)
     arrived(lc.at[1], lc_r)
     loss_ref[0, 0] = jnp.sum((lc[0] + lc[1])[0:1]) / width_all
-    g_last()
+    g_last(1)
+    g_last(0)
     ar_sent(ar_t, 0, chips)
     ar_sent(ar_p, 1, chips)
     ar_sent(ar_u, 2, chips)
@@ -846,7 +851,7 @@
     strip = wide // chips
     quarter = half // 2
     piece = quarter // nz
-    band = 7 * half // 32
+    band = half // 4
     V = pltpu.VMEM
     D = pltpu.SemaphoreType.DMA
     data = [
@@ -876,8 +881,8 @@
         V((2, nz // 2 + 1, 2, half // 2 - band, strip), F32),
         V((2, band, strip), F32),
         V((2, band, strip), F32),
-        V((strip // 2, half), F32),
-        V((strip // 2, half), F32),
+        V((2, strip // 2, quarter), F32),
+        V((2, strip // 2, quarter), F32),
         V((chips, 8, 128), F32),
         V((chips, 8, 128), F32),
         V((chips, 8, 128), F32),
@@ -893,9 +898,9 @@
         D(shape) for shape in (
             (7,), (3,), (8,), (7,),
             (2, ny), (2, 2), (), (2, 5), (), (), (), (2, 4),
-            (2, 2, nz // 2), (2,), (2, 2, nz // 2), (2, 5),
+            (2, nz // 2), (2,), (2, nz // 2), (2, 5),
             (), (2, 4), (2, 2, nz // 2), (4,), (2, 2),
-            (2, 2, nz // 2), (2,), (5,), (2, nz // 2), (), (),
+            (2, nz // 2), (2,), (5,), (nz // 2,), (2,), (),
         )
     ]
     vm = pl.BlockSpec(memory_space=pltpu.VMEM)

time: 113 us -> 115 us (1.018)
  Pallas kernels: 109 us -> 111 us
    pallas_call x1, Pallas kernels: 109 us -> 111 us  [shards(): pl.pallas_call(functools.partial(kernel, nz, ny), out_shape=(jax.ShapeDty...]
where the time goes in v6:
time: 115 us
  Pallas kernels  111 us (97%)
  between operations  2.45 us (2%)
  local copies, waits for them, and re-layouts  1.57 us (1%)
    pallas_call x1, Pallas kernels, shards(): pl.pallas_call(functools.partial(kernel, nz, ny), out_shape=(jax.ShapeDty...  111 us

profile of v6, /device:TPU:1, one launch (start us, length us, event | category | flops | bytes accessed | tf_op | source)
XLA Modules:
  0.0 114.6 jit_solution(8643037467068932402)
XLA Ops:
  0.6 110.5 %shard_map.50 = (f32[1,1]{1,0:T(1,128)}, f32[64,512]{1,0:T(8,128)}) custom-call(bf16[512,2048]{1,0:T(8,128)(2,1)} %x_hbm.1, bf16[64,512]{1,0:T(8,128)(2,1)} %w_hbm.1, bf16[512,512]{1,0:T(8,128)(2,1)} %t_hbm.1), custom_call_target="tpu_custom_call" | custom-call | tf_op jit(solution)/shard_map/pallas_call | solution.py:909
  111.9 1.6 %copy.8 = f32[64,512]{1,0:T(8,128)} copy(f32[64,512]{1,0:T(8,128)} %get-tuple-element.9) | data formatting | bytes 262144

commit v7 on v5

--- a/solution.py
+++ b/solution.py
@@ -800,15 +800,18 @@
     gradient(xl, gg, 0, 1)
     ga_step(0)
     gradient(1 - xl, gs, 1, nz // 2)
-    gb_over(1, 2, 3, 4, 5, 6, 7)
+    gb_over(1, 2)
     gradient(xl, gg, 1, nz // 2)
     lf[f] = jnp.broadcast_to(jnp.sum(sums[lanes:2 * lanes], axis=0, keepdims=True), (8, 128))
     f_start(lf, 4)
     gb_step(0)
+    gb_over(3, 4)
     ga_step(1)
     gb_step(1)
+    gb_over(5, 6)
     ga_step(2)
     gb_step(2)
+    gb_over(7)
     ga_step(3)
     gb_step(3)
     f_wait(lf, 4)

time: 113 us -> 113 us (level)
  no operation moved by 1% of the time
where the time goes in v7:
time: 113 us
  Pallas kernels  109 us (96%)
  between operations  2.45 us (2%)
  local copies, waits for them, and re-layouts  1.57 us (1%)
    pallas_call x1, Pallas kernels, shards(): pl.pallas_call(functools.partial(kernel, nz, ny), out_shape=(jax.ShapeDty...  109 us

profile of v7, /device:TPU:1, one launch (start us, length us, event | category | flops | bytes accessed | tf_op | source)
XLA Modules:
  0.0 112.9 jit_solution(144545164181464446)
XLA Ops:
  0.6 108.9 %shard_map.50 = (f32[1,1]{1,0:T(1,128)}, f32[64,512]{1,0:T(8,128)}) custom-call(bf16[512,2048]{1,0:T(8,128)(2,1)} %x_hbm.1, bf16[64,512]{1,0:T(8,128)(2,1)} %w_hbm.1, bf16[512,512]{1,0:T(8,128)(2,1)} %t_hbm.1), custom_call_target="tpu_custom_call" | custom-call | tf_op jit(solution)/shard_map/pallas_call | solution.py:907
  110.2 1.6 %copy.8 = f32[64,512]{1,0:T(8,128)} copy(f32[64,512]{1,0:T(8,128)} %get-tuple-element.9) | data formatting | bytes 262144
